TPU v7x, 32 devices: a whole 2x2x4 slice. The times are simulated.
32 devices in a mesh: sp: 8 (over y, x, core), dp: 4 (over z).
Axes of the slice: x: 2, y: 2, z: 4, core: 2. Of those that a mesh axis runs over, the one named last changes fastest.
Arguments:
- tokens: bfloat16 [16, 1024, 1536], P('dp', 'sp'), may hold values from -6 to 6
- norm_gain: bfloat16 [1536], P('sp'), may hold values from 0.099609375 to 1.8984375
- in_weight: bfloat16 [1536, 6400], P('sp'), may hold values from -0.15625 to 0.15625
- step_weight: bfloat16 [1536, 48], P('sp'), may hold values from -0.15625 to 0.15625
- filter_weight: bfloat16 [4, 3328], P(None, 'sp'), may hold values from -3 to 3
- filter_bias: bfloat16 [3328], P('sp'), may hold values from -3 to 3
- step_bias: bfloat16 [48], P('sp'), may hold values from -5.5 to -3.5
- log_rate: bfloat16 [48], P('sp'), may hold values from -9 to 2
- skip_scale: bfloat16 [48], P('sp'), may hold values from 0.5 to 1.5
- inner_gain: bfloat16 [3072], P('sp'), may hold values from 0.099609375 to 1.8984375
- out_weight: bfloat16 [3072, 1536], P('sp'), may hold values from -0.109375 to 0.109375
- cotangent: bfloat16 [16, 1024, 1536], P('dp', 'sp'), may hold values from -6 to 6
Outputs:
- output: bfloat16 [16, 1024, 1536], P('dp', 'sp')
- token_gradient: float32 [16, 1024, 1536], P('dp', 'sp')
- norm_gain_gradient: float32 [1536], P('sp')
- in_gradient: float32 [1536, 6400], P('sp')
- step_gradient: float32 [1536, 48], P('sp')
- filter_gradient: float32 [4, 3328], P(None, 'sp')
- filter_bias_gradient: float32 [3328], P('sp')
- step_bias_gradient: float32 [48], P('sp')
- rate_gradient: float32 [48], P('sp')
- skip_gradient: float32 [48], P('sp')
- inner_gain_gradient: float32 [3072], P('sp')
- out_gradient: float32 [3072, 1536], P('sp')
All inputs are finite; a program needn't handle non-finite values.
Results may differ from a plain program's by a relative error of at most 0.0076.
Values may be sent and summed in bfloat16 or wider, within the bound.
No kernel may reach another device: no remote copies, remote signals or barrier semaphores. Data moves between devices by JAX's collectives and lax.ppermute only.
A program may use at most 384 MiB of HBM per device.

v0:
```python
import jax
import jax.numpy as jnp
from jax import lax
from jax.sharding import PartitionSpec as P

N = 128


EPSILON = 1e-05
precise = lax.Precision.HIGHEST


def shifted(block, axis, distance):
    devices = range(lax.axis_size(axis))
    route = [(i - distance, i) for i in devices if i - distance in devices]
    return lax.ppermute(block, axis, route)


def carried_in(shard, axis, combine, identity, reverse):
    count, place = (lax.axis_size(axis), lax.axis_index(axis))
    everything = jax.tree.map(lambda part: lax.all_gather(part, axis), shard)
    start = jax.tree.map(
        lambda part, zero: jnp.broadcast_to(jnp.asarray(zero, part.dtype), part.shape),
        shard,
        identity,
    )

    def hop(k, before):
        at = count - 1 - k if reverse else k
        reached = at > place if reverse else at < place
        new = combine(before, jax.tree.map(lambda part: part[at], everything))
        return jax.tree.map(lambda a, b: jnp.where(reached, a, b), new, before)

    return lax.fori_loop(0, count, hop, start)


def scale_rows(value_rows, gain):
    return (
        value_rows
        * lax.rsqrt(jnp.mean(value_rows * value_rows, axis=-1, keepdims=True) + EPSILON)
        * gain
    )


def block_out(signal, steps, entry, readout, rate, skip_scale, state):
    running = jnp.cumsum(steps * rate, axis=0)
    width = signal.shape[0]
    rows = lax.broadcasted_iota(jnp.int32, (width, width), 0)
    cols = lax.broadcasted_iota(jnp.int32, (width, width), 1)
    below = (cols <= rows)[:, :, None]
    spans = jnp.where(below, running[:, None, :] - running[None, :, :], -1e30)
    kernel = jnp.exp(spans)
    intersection = jnp.dot(readout, entry.T, precision=precise)
    mixing = kernel * intersection[:, :, None] * steps[None, :, :]
    result = jnp.einsum("tsh,shp->thp", mixing, signal, precision=precise)
    carried = jnp.einsum("tn,hpn->thp", readout, state, precision=precise)
    result = result + jnp.exp(running)[:, :, None] * carried + skip_scale[None, :, None] * signal
    remaining = jnp.exp(running[-1:, :] - running) * steps
    updated = jnp.exp(running[-1, :])[:, None, None] * state
    updated = updated + jnp.einsum("sh,shp,sn->hpn", remaining, signal, entry, precision=precise)
    return (result, updated)


def run_blocks(signal, steps, entry, readout, rate, skip_scale, state, width):
    length, heads, size = signal.shape
    count = length // width
    items = (
        signal.reshape(count, width, heads, size),
        steps.reshape(count, width, heads),
        entry.reshape(count, width, entry.shape[1]),
        readout.reshape(count, width, readout.shape[1]),
    )

    def run_advance(carry, block):
        result, updated = block_out(block[0], block[1], block[2], block[3], rate, skip_scale, carry)
        return (updated, result)

    final, results = lax.scan(jax.checkpoint(run_advance), state, items)
    return (results.reshape(length, heads, size), final)


def block_state(signal, steps, entry, rate, state):
    running = jnp.cumsum(steps * rate, axis=0)
    remaining = jnp.exp(running[-1:, :] - running) * steps
    updated = jnp.exp(running[-1, :])[:, None, None] * state
    return updated + jnp.einsum("sh,shp,sn->hpn", remaining, signal, entry, precision=precise)


def local_states(signal, steps, entry, rate, width):
    length, heads, size = signal.shape
    count = length // width
    items = (
        signal.reshape(count, width, heads, size),
        steps.reshape(count, width, heads),
        entry.reshape(count, width, entry.shape[1]),
    )

    def local_advance(carry, block):
        return (block_state(block[0], block[1], block[2], rate, carry), None)

    start = jnp.zeros((heads, size, entry.shape[1]), jnp.float32)
    final, _ = lax.scan(jax.checkpoint(local_advance), start, items)
    return final


def prepare(mixed_in, edge, raw_steps, filter_weight, filter_bias, step_bias, log_rate):
    length = mixed_in.shape[0]
    taps = filter_weight.shape[0]
    padded = jnp.concatenate([edge, mixed_in], axis=0)
    filtered = filter_bias
    for tap in range(taps):
        filtered = filtered + filter_weight[tap] * padded[tap : tap + length]
    active = jax.nn.silu(filtered)
    inner = active.shape[1] - 2 * N
    heads = log_rate.shape[0]
    signal = active[:, :inner].reshape(length, heads, inner // heads)
    entry = active[:, inner : inner + N]
    readout = active[:, inner + N :]
    steps = jax.nn.softplus(raw_steps + step_bias)
    rate = -jnp.exp(log_rate)
    local = local_states(signal, steps, entry, rate, min(length, 256))
    decay = jnp.exp(jnp.sum(steps * rate, axis=0))
    return (signal, entry, readout, steps, decay, local)


def finish(signal, entry, readout, steps, gate, incoming, log_rate, skip_scale, inner_gain):
    rate = -jnp.exp(log_rate)
    result, _ = run_blocks(
        signal, steps, entry, readout, rate, skip_scale, incoming, min(signal.shape[0], 256)
    )
    gated = result.reshape(gate.shape) * jax.nn.silu(gate)
    return scale_rows(gated, inner_gain)


def forward_join(earlier, later):
    return (earlier[0] * later[0], later[0][:, :, None, None] * earlier[1] + later[1])


def backward_join(earlier, later):
    return (later[0] * earlier[0], later[1] + later[0][:, :, None, None] * earlier[1])


def body(
    tokens,
    norm_gain,
    in_weight,
    step_weight,
    filter_weight,
    filter_bias,
    step_bias,
    log_rate,
    skip_scale,
    inner_gain,
    out_weight,
    cotangent,
):
    (
        whole_gain,
        gathered_input_weight,
        gathered_step_weight,
        whole_filter,
        whole_fbias,
        whole_sbias,
        whole_rate,
        whole_skip,
        whole_inner,
        gathered_output_weight,
    ) = (
        lax.all_gather(norm_gain, "sp", axis=0, tiled=True),
        lax.all_gather(in_weight, "sp", axis=0, tiled=True),
        lax.all_gather(step_weight, "sp", axis=0, tiled=True),
        lax.all_gather(filter_weight, "sp", axis=1, tiled=True),
        lax.all_gather(filter_bias, "sp", axis=0, tiled=True),
        lax.all_gather(step_bias, "sp", axis=0, tiled=True),
        lax.all_gather(log_rate, "sp", axis=0, tiled=True),
        lax.all_gather(skip_scale, "sp", axis=0, tiled=True),
        lax.all_gather(inner_gain, "sp", axis=0, tiled=True),
        lax.all_gather(out_weight, "sp", axis=0, tiled=True),
    )
    value_rows = tokens.astype(jnp.float32)
    normed, norm_pull = jax.vjp(scale_rows, value_rows, whole_gain.astype(jnp.float32))
    normalized_lower = normed.astype(jnp.bfloat16)
    projected_rows = jnp.einsum(
        "ofh,hc->ofc", normalized_lower, gathered_input_weight, preferred_element_type=jnp.float32
    )
    raw_steps = jnp.einsum(
        "ftb,bp->ftp", normalized_lower, gathered_step_weight, preferred_element_type=jnp.float32
    )
    inner = whole_inner.shape[0]
    gate = projected_rows[:, :, :inner]
    mixed_in = projected_rows[:, :, inner:]
    taps = whole_filter.shape[0]
    length = mixed_in.shape[1]
    edge = shifted(mixed_in[:, length - taps + 1 :, :], "sp", 1)
    prepared, prepare_pull = jax.vjp(
        jax.vmap(prepare, in_axes=(0, 0, 0, None, None, None, None)),
        mixed_in,
        edge,
        raw_steps,
        whole_filter.astype(jnp.float32),
        whole_fbias.astype(jnp.float32),
        whole_sbias.astype(jnp.float32),
        whole_rate.astype(jnp.float32),
    )
    signal, entry, readout, steps, decay, local = prepared
    neutral = (jnp.ones_like(decay), jnp.zeros_like(local))
    incoming = carried_in((decay, local), "sp", forward_join, neutral, False)[1]
    mixed_out, finish_pull = jax.vjp(
        jax.vmap(finish, in_axes=(0, 0, 0, 0, 0, 0, None, None, None)),
        signal,
        entry,
        readout,
        steps,
        gate,
        incoming,
        whole_rate.astype(jnp.float32),
        whole_skip.astype(jnp.float32),
        whole_inner.astype(jnp.float32),
    )
    mixed_lower_precision = mixed_out.astype(jnp.bfloat16)
    output = (
        value_rows
        + jnp.einsum(
            "vbo,ot->vbt",
            mixed_lower_precision,
            gathered_output_weight,
            preferred_element_type=jnp.float32,
        )
    ).astype(jnp.bfloat16)
    backward_input_weight, backward_step_weight, backward_output_weight = (
        lax.all_gather(in_weight, "sp", axis=0, tiled=True),
        lax.all_gather(step_weight, "sp", axis=0, tiled=True),
        lax.all_gather(out_weight, "sp", axis=0, tiled=True),
    )
    output_weight_gradient = jnp.einsum(
        "rpi,rph->ih", mixed_lower_precision, cotangent, preferred_element_type=jnp.float32
    )
    mixed_gradient = jnp.einsum(
        "puc,ac->pua", cotangent, backward_output_weight, preferred_element_type=jnp.float32
    )
    g_signal, g_entry, g_readout, g_steps, g_gate, g_incoming, rate_late, grad_skip, grad_inner = (
        finish_pull(mixed_gradient)
    )
    returning = carried_in((decay, g_incoming), "sp", backward_join, neutral, True)[1]
    g_decay = jnp.sum(returning * incoming, axis=(2, 3))
    g_mixed_in, g_edge, g_raw, grad_filter, grad_fbias, grad_sbias, rate_early = prepare_pull(
        (g_signal, g_entry, g_readout, g_steps, g_decay, returning)
    )
    edge_back = shifted(g_edge.astype(jnp.bfloat16), "sp", -1).astype(g_edge.dtype)
    g_mixed_in = jnp.concatenate(
        [g_mixed_in[:, : length - taps + 1, :], g_mixed_in[:, length - taps + 1 :, :] + edge_back],
        axis=1,
    )
    projected_gradient = jnp.concatenate([g_gate, g_mixed_in], axis=2).astype(jnp.bfloat16)
    raw_lower_gradient = g_raw.astype(jnp.bfloat16)
    input_weight_gradient = jnp.einsum(
        "gza,gzc->ac", normalized_lower, projected_gradient, preferred_element_type=jnp.float32
    )
    step_weight_grad = jnp.einsum(
        "apo,apc->oc", normalized_lower, raw_lower_gradient, preferred_element_type=jnp.float32
    )
    normalized_gradient = jnp.einsum(
        "ivg,ug->ivu", projected_gradient, backward_input_weight, preferred_element_type=jnp.float32
    )
    normalized_gradient = normalized_gradient + jnp.einsum(
        "uva,ka->uvk", raw_lower_gradient, backward_step_weight, preferred_element_type=jnp.float32
    )
    g_values, grad_gain = norm_pull(normalized_gradient)
    token_gradient = cotangent.astype(jnp.float32) + g_values
    (
        part_gain,
        part_in,
        part_step,
        part_filter,
        part_fbias,
        part_sbias,
        part_rate,
        part_skip,
        part_inner,
        part_out,
    ) = (
        lax.psum_scatter(grad_gain, "sp", scatter_dimension=0, tiled=True),
        lax.psum_scatter(input_weight_gradient, "sp", scatter_dimension=0, tiled=True),
        lax.psum_scatter(step_weight_grad, "sp", scatter_dimension=0, tiled=True),
        lax.psum_scatter(grad_filter, "sp", scatter_dimension=1, tiled=True),
        lax.psum_scatter(grad_fbias, "sp", scatter_dimension=0, tiled=True),
        lax.psum_scatter(grad_sbias, "sp", scatter_dimension=0, tiled=True),
        lax.psum_scatter(rate_early + rate_late, "sp", scatter_dimension=0, tiled=True),
        lax.psum_scatter(grad_skip, "sp", scatter_dimension=0, tiled=True),
        lax.psum_scatter(grad_inner, "sp", scatter_dimension=0, tiled=True),
        lax.psum_scatter(output_weight_gradient, "sp", scatter_dimension=0, tiled=True),
    )
    (
        total_gain,
        total_in,
        total_step,
        total_filter,
        total_fbias,
        total_sbias,
        total_rate,
        total_skip,
        total_inner,
        total_out,
    ) = lax.psum(
        (
            part_gain,
            part_in,
            part_step,
            part_filter,
            part_fbias,
            part_sbias,
            part_rate,
            part_skip,
            part_inner,
            part_out,
        ),
        "dp",
    )
    return (
        output,
        token_gradient,
        total_gain,
        total_in,
        total_step,
        total_filter,
        total_fbias,
        total_sbias,
        total_rate,
        total_skip,
        total_inner,
        total_out,
    )


def solution(mesh):
    return jax.shard_map(
        body,
        mesh=mesh,
        in_specs=(
            P("dp", "sp", None),
            P("sp"),
            P("sp", None),
            P("sp", None),
            P(None, "sp"),
            P("sp"),
            P("sp"),
            P("sp"),
            P("sp"),
            P("sp"),
            P("sp", None),
            P("dp", "sp", None),
        ),
        out_specs=(
            P("dp", "sp", None),
            P("dp", "sp", None),
            P("sp"),
            P("sp", None),
            P("sp", None),
            P(None, "sp"),
            P("sp"),
            P("sp"),
            P("sp"),
            P("sp"),
            P("sp"),
            P("sp", None),
        ),
        check_vma=False,
    )
```

profile of v0, /device:TPU:0, one launch (start us, length us, event | category | flops | bytes accessed | tf_op | source)
XLA Modules:
  0.0 1559.9 jit_solution(7364277992526796824)
XLA Ops:
  15.5 26.2 %all-reduce.29 = (bf16[1536]{0:T(1024)(128)(2,1)S(1)}, bf16[3328]{0:T(1024)(128)(2,1)S(1)}, bf16[48]{0:T(256)(128)(2,1)S(1)}, bf16[48]{0:T(256)(128)(2,1)S(1)}, bf16[48]{0:T(256)(128)(2,1)S(1)}) all-reduce(bf16[1536]{0:T(1024)(128)(2,1)S(1)} %dynamic-update-slice.1, ...), channel_id=1, replica_groups=mesh['sp'=8,'dp'=4] {'sp'}, use_global_device_ids=true, to_apply=%add.16 | all-reduce | flops 5008 | bytes 20032
  65.9 49.9 %all-gather.12.cloned.1.call-done = bf16[1536,6400]{1,0:T(8,128)(2,1)} async-done(((bf16[192,6400]{1,0:T(8,128)(2,1)}), bf16[1536,6400]{1,0:T(8,128)(2,1)}) %all-gather.12.cloned.1.call-update) | async-done | bytes 19660816 | tf_op jit(solution)/shard_map/all_gather | solution.py:170
  115.8 13.4 fusion.4
  193.8 28.2 %fusion.11 = f32[4,48,64,128]{3,2,1,0:T(8,128)} fusion(f32[4,128,48,64]{1,3,2,0:T(8,128)} %bitcast.177, f32[4,128,48]{1,2,0:T(8,128)S(1)} %copy.174, f32[4,128,128]{2,1,0:T(8,128)S(1)} %fusion.129, f32[4,128,48]{1,2,0:T(8,128)S(1)} %copy.172, pred[128,128]{1,0:T(8,128)(4,1)S(1)} %iota_compare_fusion), kind=kOutput, calls=%fused_computation.21 | convolution fusion | flops 2428502016 | bytes 13058048 | tf_op jit(solution)/shard_map/jvp(vmap())/while/body/eval_jaxpr/tsh,shp->thp/dot_general | solution.py:55
  222.0 183.3 %all-gather.16.cloned.1.call-done = f32[32,48,64,128]{3,2,1,0:T(8,128)} async-done(((f32[4,48,64,128]{3,2,1,0:T(8,128)}), f32[32,48,64,128]{3,2,1,0:T(8,128)}) %all-gather.16.cloned.1.call-update) | async-done | bytes 50331664 | tf_op jit(solution)/shard_map/all_gather | solution.py:21
  405.3 64.9 %while.20 = (s32[]{:T(128)}, f32[4,48,64,128]{3,2,1,0:T(8,128)}, s32[]{:T(128)}, f32[8,4,48]{2,1,0:T(4,128)S(1)}, f32[8,4,48,64,128]{4,3,2,1,0:T(8,128)}, /*index=5*/s32[]{:T(128)}, s32[]{:T(128)}) while((s32[]{:T(128)}, f32[4,48,64,128]{3,2,1,0:T(8,128)}, s32[]{:T(128)}, f32[8,4,48]{2,1,0:T(4,128)S(1)}, ...), condition=%wide.region_4.5_spmd.clone, body=%wide.region_3.4_spmd.clone.sunk | while | flops 6291460 | bytes 18876784 | solution.py:34
  470.3 11.8 fusion.35
  553.7 16.4 %convolution_bitcast_fusion.1 = f32[3072,1536]{1,0:T(8,128)} fusion(bf16[4,128,1536]{2,1,0:T(8,128)(2,1)S(1)} %copy-done.16, f32[4,128,3072]{2,1,0:T(8,128)} %get-tuple-element.512, f32[3072]{0:T(1024)S(1)} %bitcast.211, f32[4,128]{1,0:T(4,128)S(1)} %copy-done.60), kind=kOutput, calls=%fused_computation.11 | convolution fusion | flops 4836556800 | bytes 26753024 | tf_op jit(solution)/shard_map/rpi,rph->ih/dot_general | solution.py:235
  571.2 13.7 fusion.89
  584.9 31.7 %fusion.22 = (f32[4,128,48]{1,2,0:T(8,128)}, f32[4,128,48]{1,2,0:T(8,128)}, f32[4,128,48]{1,2,0:T(8,128)}, f32[4,128,128]{2,1,0:T(8,128)S(1)}) fusion(f32[4,128,128]{2,1,0:T(8,128)S(1)} %fusion.143, f32[4,128,48]{1,2,0:T(8,128)S(1)} %copy.186, f32[4,128,48]{1,2,0:T(8,128)S(1)} %copy.184, pred[128,128]{1,0:T(8,128)(4,1)S(1)} %iota_compare_fusion, ...), kind=kOutput, calls=%fused_computation.37 | convolution fusion | flops 2456674304 | bytes 13615104 | tf_op jit(solution)/shard_map/transpose(jvp(vmap()))/while/body/eval_jaxpr/checkpoint/tsh,shp->thp/dot_general | solution.py:55
  617.7 11.1 fusion.92
  628.8 155.9 %all-gather.18.cloned.1.call-done = f32[32,48,64,128]{3,2,1,0:T(8,128)} async-done(((f32[4,48,64,128]{3,2,1,0:T(8,128)}), f32[32,48,64,128]{3,2,1,0:T(8,128)}) %all-gather.18.cloned.1.call-update) | async-done | bytes 50331664 | tf_op jit(solution)/shard_map/all_gather | solution.py:21
  784.7 72.0 %while.21 = (s32[]{:T(128)}, f32[4,48,64,128]{3,2,1,0:T(8,128)}, s32[]{:T(128)}, f32[8,4,48,64,128]{4,3,2,1,0:T(8,128)}, f32[8,4,48]{2,1,0:T(4,128)S(1)}, /*index=5*/s32[]{:T(128)}, s32[]{:T(128)}, s32[]{:T(128)}, s32[]{:T(128)}) while((s32[]{:T(128)}, f32[4,48,64,128]{3,2,1,0:T(8,128)}, s32[]{:T(128)}, ...), condition=%wide.region_10.11_spmd.clone, body=%wide.region_9.10_spmd.clone.sunk | while | flops 6291464 | bytes 18876848 | solution.py:34
  801.4 11.4 fusion.169
  874.5 19.6 %fusion.31 = f32[4,128,48,64]{1,3,2,0:T(8,128)} fusion(f32[4,128,48,64]{1,3,2,0:T(8,128)} %get-tuple-element.542, f32[4,128,48,64]{1,3,2,0:T(8,128)} %bitcast.193, f32[4,128,48,64]{1,3,2,0:T(8,128)} %get-tuple-element.540, f32[4,128,128]{2,1,0:T(8,128)S(1)} %fusion.143, f32[4,128,48]{1,2,0:T(8,128)S(1)} %copy.186, f32[4,128,48]{1,2,0:T(8,128)S(1)} %copy.184, ...), kind=kOutput, calls=%fused_computation.58 | convolution fusion | flops 2437939200 | bytes 25837760 | tf_op jit(solution)/shard_map/transpose(jvp(vmap()))/while/body/eval_jaxpr/checkpoint/tsh,shp->thp/dot_general | solution.py:55
  901.1 14.2 fusion.95
  916.1 11.4 multiply_reduce_fusion.3
  949.9 21.1 %convolution_bitcast_fusion = f32[1536,6400]{1,0:T(8,128)} fusion(bf16[4,3,3328]{2,1,0:T(4,128)(2,1)S(1)} %fusion.117, bf16[4,125,3328]{2,1,0:T(8,128)(2,1)} %slice.102, bf16[4,128,3072]{2,1,0:T(8,128)(2,1)} %get-tuple-element.518, bf16[4,128,1536]{2,1,0:T(8,128)(2,1)S(1)} %copy-done.6, f32[1536]{0:T(1024)S(1)} %copy-done.30, f32[4,128]{1,0:T(4,128)S(1)} %copy-done.34), kind=kOutput, calls=%fused_computation.6 | convolution fusion | flops 10089136128 | bytes 47456256 | tf_op jit(solution)/shard_map/gza,gzc->ac/dot_general | solution.py:256
  1010.0 195.1 %reduce-scatter.9.cloned.1.call-done = f32[192,6400]{1,0:T(8,128)} async-done(((f32[1536,6400]{1,0:T(8,128)}), f32[192,6400]{1,0:T(8,128)}) %reduce-scatter.9.cloned.1.call-update) | async-done | bytes 4915216 | tf_op jit(solution)/shard_map/reduce_scatter | solution.py:283
  1221.0 27.4 %reduce-scatter.15.cloned.1.call-done = f32[416,4]{1,0:T(8,128)} async-done(((f32[3328,4]{1,0:T(8,128)}), f32[416,4]{1,0:T(8,128)}) %reduce-scatter.15.cloned.1.call-update) | async-done | bytes 6672
  1249.5 17.6 %fusion.71 = (f32[1536]{0:T(1024)S(1)}, f32[4,128]{1,0:T(4,128)S(1)}, f32[4,128,1536]{2,1,0:T(8,128)}) fusion(bf16[4,128,1536]{2,1,0:T(8,128)(2,1)S(1)} %copy-done.6, f32[4,128]{1,0:T(4,128)S(1)} %copy-done.34, f32[1536]{0:T(1024)S(1)} %copy-done.30, f32[4,128,1536]{2,1,0:T(8,128)} %fusion.144, bf16[1536,6400]{1,0:T(8,128)(2,1)} %all-gather.12.cloned.1.call-done, ...), kind=kOutput, calls=%fused_computation.114 | convolution fusion | flops 10092279808 | bytes 34095104 | tf_op jit(solution)/shard_map/ivg,ug->ivu/dot_general | solution.py:262
  1267.1 23.7 %all-reduce.26 = (f32[1536]{0:T(1024)S(1)}, f32[3328]{0:T(1024)S(1)}, f32[48]{0:T(128)S(1)}, f32[48]{0:T(128)S(1)}, f32[48]{0:T(128)S(1)}, /*index=5*/f32[3072]{0:T(1024)S(1)}) all-reduce(f32[1536]{0:T(1024)S(1)} %get-tuple-element.457, f32[3328]{0:T(1024)S(1)} %copy-done.45, ...), channel_id=5, replica_groups=mesh['sp'=8,'dp'=4] {'sp'}, use_global_device_ids=true, to_apply=%region_25.26.clone | all-reduce | flops 8080 | bytes 64640
  1297.1 26.4 %all-reduce.27 = (f32[192]{0:T(256)}, f32[192,48]{0,1:T(8,128)}, f32[4,416]{1,0:T(4,128)}, f32[416]{0:T(512)}, f32[6]{0:T(128)}, /*index=5*/f32[6]{0:T(128)}, f32[6]{0:T(128)}, f32[384]{0:T(512)}) all-reduce(f32[192]{0:T(256)S(1)} %dynamic-slice.13, f32[192,48]{0,1:T(8,128)S(1)} %copy.232, ...), channel_id=1, replica_groups=mesh['sp'=8,'dp'=4] {'dp'}, use_global_device_ids=true, to_apply=%region_26.27 | all-reduce | flops 11890 | bytes 95120 | tf_op jit(solution)/shard_map/psum | solution.py:304
  1323.5 222.9 %all-reduce.32.cloned.1.call-done = (f32[192,6400]{1,0:T(8,128)}, f32[384,1536]{1,0:T(8,128)}) async-done(((f32[192,6400]{1,0:T(8,128)}, f32[384,1536]{1,0:T(8,128)}), (f32[192,6400]{1,0:T(8,128)}, f32[384,1536]{1,0:T(8,128)})) %all-reduce.32.cloned.1.call-update) | async-done | bytes 7274512 | tf_op jit(solution)/shard_map/psum | solution.py:304
  (373 shorter events, 407.3 us)
Async XLA Ops:
  7.2 108.6 %copy-start.5 = (bf16[4,128,1536]{2,1,0:T(8,128)(2,1)S(1)}, bf16[4,128,1536]{2,1,0:T(8,128)(2,1)}, u32[]{:S(2)}) copy-start(bf16[4,128,1536]{2,1,0:T(8,128)(2,1)} %param.16) | copy-start | bytes 4718596
  7.2 49.6 %copy-start.64 = (bf16[4,416]{1,0:T(4,128)(2,1)S(1)}, bf16[4,416]{1,0:T(4,128)(2,1)}, u32[]{:S(2)}) copy-start(bf16[4,416]{1,0:T(4,128)(2,1)} %param.20) | copy-start | bytes 9988
  7.2 108.6 %all-gather.12.cloned.1.call-start = ((), (), s32[]{:S(2)}) async-start(), calls=%async_computation.4 | async-start | bytes 22118400 | tf_op jit(solution)/shard_map/all_gather | solution.py:170
  7.9 397.4 %all-gather.16.cloned.1.call-start = ((), (), s32[]{:S(2)}) async-start(), calls=%async_computation.8 | async-start | bytes 56623104 | tf_op jit(solution)/shard_map/all_gather | solution.py:21
  41.8 87.5 %copy-start.29 = (f32[1536]{0:T(1024)}, f32[1536]{0:T(1024)S(1)}, u32[]{:S(2)}) copy-start(f32[1536]{0:T(1024)S(1)} %convert_element_type.48) | copy-start | bytes 18436
  53.6 75.7 %copy-start.33 = (f32[4,128]{1,0:T(4,128)}, f32[4,128]{1,0:T(4,128)S(1)}, u32[]{:S(2)}) copy-start(f32[4,128]{1,0:T(4,128)S(1)} %fusion.120) | copy-start | bytes 6148
  55.8 73.4 %copy-start.66 = (f32[48]{0:T(128)}, f32[48]{0:T(128)S(1)}, u32[]{:S(2)}) copy-start(f32[48]{0:T(128)S(1)} %convert_element_type.50) | copy-start | bytes 580
  55.9 800.8 %copy-start.50 = (f32[48]{0:T(128)}, f32[48]{0:T(128)S(1)}, u32[]{:S(2)}) copy-start(f32[48]{0:T(128)S(1)} %fusion.122) | copy-start | bytes 580
  56.2 126.6 %copy-start.54 = (f32[4,48]{1,0:T(4,128)}, f32[4,48]{1,0:T(4,128)S(1)}, u32[]{:S(2)}) copy-start(f32[4,48]{1,0:T(4,128)S(1)} %get-tuple-element.513) | copy-start | bytes 2308
  134.1 6.6 collective-permute-start
  172.8 323.4 %all-gather.14.cloned.1.call-start = ((), (), s32[]{:S(2)}) async-start(), calls=%async_computation.5 | async-start | bytes 10616832 | tf_op jit(solution)/shard_map/all_gather | solution.py:178
  173.5 611.1 %all-gather.18.cloned.1.call-start = ((), (), s32[]{:S(2)}) async-start(), calls=%async_computation.9 | async-start | bytes 56623104 | tf_op jit(solution)/shard_map/all_gather | solution.py:21
  173.9 296.4 %copy-start.73 = (f32[48]{0:T(128)}, f32[48]{0:T(128)S(1)}, u32[]{:S(2)}) copy-start(f32[48]{0:T(128)S(1)} %convert_element_type.52) | copy-start | bytes 580
  182.9 369.5 %copy-start.46 = (f32[8,1,384]{2,1,0:T(1,128)}, f32[8,1,384]{2,1,0:T(1,128)S(1)}, u32[]{:S(2)}) copy-start(f32[8,1,384]{2,1,0:T(1,128)S(1)} %convert_element_type.60) | copy-start | bytes 36868
  552.3 457.7 %reduce-scatter.11.cloned.1.call-start = ((), (), s32[]{:S(2)}) async-start(), calls=%async_computation.7 | async-start | bytes 21233664 | tf_op jit(solution)/shard_map/reduce_scatter | solution.py:291
  570.1 635.0 %reduce-scatter.9.cloned.1.call-start = ((), (), s32[]{:S(2)}) async-start(), calls=%async_computation.6 | async-start | bytes 44236800 | tf_op jit(solution)/shard_map/reduce_scatter | solution.py:283
  571.1 46.5 %slice-start.2 = ((s8[6291456]{0:T(1024)(128)(4,1)}), s8[4194304]{0:T(1024)(128)(4,1)S(1)}, s32[]{:S(2)}) async-start(s8[6291456]{0:T(1024)(128)(4,1)} %bitcast.185), calls=%async_computation.15 | async-start | bytes 8388608
  571.2 46.5 %slice-start.4 = ((s8[6291456]{0:T(1024)(128)(4,1)}), s8[4194304]{0:T(1024)(128)(4,1)S(1)}, s32[]{:S(2)}) async-start(s8[6291456]{0:T(1024)(128)(4,1)} %bitcast.188), calls=%async_computation.17 | async-start | bytes 8388608
  942.9 5.9 collective-permute-start.1
  971.0 277.4 %reduce-scatter.15.cloned.1.call-start = ((), (), s32[]{:S(2)}) async-start(), calls=%async_computation.11 | async-start | bytes 1916928
  1008.0 199.7 %copy-start.47 = (f32[8,1,384]{2,1,0:T(1,128)S(1)}, f32[8,1,384]{2,1,0:T(1,128)}, u32[]{:S(2)}) copy-start(f32[8,1,384]{2,1,0:T(1,128)} %copy-done.46) | copy-start | bytes 36868
  1008.0 199.7 %copy-start.61 = (f32[4,128]{1,0:T(4,128)S(1)}, f32[4,128]{1,0:T(4,128)}, u32[]{:S(2)}) copy-start(f32[4,128]{1,0:T(4,128)} %copy-done.59) | copy-start | bytes 6148
  1008.0 288.1 %reduce-scatter.13.cloned.1.call-start = ((), (), s32[]{:S(2)}) async-start(), calls=%async_computation.10 | async-start | bytes 884736
  1009.9 536.4 %all-reduce.32.cloned.1.call-start = ((), (), s32[]{:S(2)}) async-start(), calls=%async_computation.12 | async-start | bytes 14548992 | tf_op jit(solution)/shard_map/psum | solution.py:304
  (76 other events, 873.4 us)
Sparse Core Ops, SparseCore 0:
  9.9 105.8 all-gather.11
  172.9 232.3 all-gather.15
  407.2 58.8 all-gather.13
  552.4 232.2 all-gather.17
  788.1 126.1 reduce-scatter.10
  971.1 233.9 reduce-scatter.8
  1209.4 39.0 reduce-scatter.14
  1251.6 35.0 reduce-scatter.12
  1289.2 257.1 all-reduce.31
where the time goes:
time: 1570 us; the launch traced here: 1560 us
  waiting for transfers between devices  836 us (53%)
  matrix products  279 us (18%)
  other arithmetic  230 us (15%)
  blocking collectives  111 us (7%)
  local copies, waits for them, and re-layouts  79.7 us (5%)
  between operations  20.2 us (1%)
    all_gather x2, waiting for transfers between devices, carried_in(): everything = jax.tree.map(lambda part: lax.all_gather(part, axis), shard)  339 us
    psum x1, waiting for transfers between devices, body(): lax.psum((part_gain, part_in, part_step, part_filter, part_fbias, part_sb...  223 us
    reduce_scatter x1, waiting for transfers between devices, body(): lax.psum_scatter(input_weight_gradient, 'sp', scatter_dimension=0, tiled=...  195 us
    select_n x16, other arithmetic, hop(): return jax.tree.map(lambda a, b: jnp.where(reached, a, b), new, before)  137 us
    dot_general x3, matrix products, block_out(): result = jnp.einsum('tsh,shp->thp', mixing, signal, precision=precise)  79.4 us
    unnamed x2, blocking collectives  49.9 us
    all_gather x1, waiting for transfers between devices, body(): lax.all_gather(in_weight, 'sp', axis=0, tiled=True)  49.9 us
    dot_general x4, matrix products, block_out(): carried = jnp.einsum('tn,hpn->thp', readout, state, precision=precise)  45.1 us
  transfers between devices with their start and end apart: 11, of which 6 were waited for; matrix products, arithmetic and copies ran while one was open for 30% of the time, Pallas kernels for 0%

commit v1 on v0

v1 whole, which is shorter than its diff:
```python
import jax
import jax.numpy as jnp
from jax import lax
from jax.experimental import pallas as pl
from jax.experimental.pallas import tpu as pltpu
from jax.sharding import Mesh, PartitionSpec as P

N = 128
HEAD = 64
LANES = 128
VMEM = 60 * 1024 * 1024
EPSILON = 1e-05
f32, bf16 = jnp.float32, jnp.bfloat16
precise = lax.Precision.HIGHEST


def sigmoid(v):
    return 0.5 * jnp.tanh(0.5 * v) + 0.5


def dot(a, b):
    return jnp.dot(a, b, preferred_element_type=f32)


def dot_nt(a, b):
    return lax.dot_general(a, b, (((1,), (1,)), ((), ())), preferred_element_type=f32)


def spread_pair(low, a, p):
    return jnp.where(low, a[:, 2 * p : 2 * p + 1], a[:, 2 * p + 1 : 2 * p + 2])


def stacked(low, a):
    zero = jnp.zeros_like(a)
    return jnp.concatenate([jnp.where(low, a, zero), jnp.where(low, zero, a)], axis=0).astype(bf16)


def running_sum(x):
    rows = lax.broadcasted_iota(jnp.int32, x.shape, 0)
    k = 1
    while k < x.shape[0]:
        x = x + jnp.where(rows >= k, pltpu.roll(x, k, 0), 0.0)
        k *= 2
    return x


def forward_kernel(
    rank, projected, by_channel, by_head, result, scaled, squares, states, state, window
):
    step = pl.program_id(0)
    width, local = result.shape
    channels = local + 2 * N
    taps = 4

    @pl.when(step == 0)
    def _():
        state[...] = jnp.zeros_like(state)
        window[0:8, :] = jnp.zeros((8, channels), f32)

    @pl.when(step > 0)
    def _():
        window[0:8, :] = window[width : width + 8, :]

    window[8 : 8 + width, :] = projected[:, local : local + channels]
    filtered = by_channel[4:5, :]
    for tap in range(taps):
        at = 9 - taps + tap
        filtered = filtered + by_channel[tap : tap + 1, :] * window[at : at + width, :]
    active = filtered * sigmoid(filtered)
    entry = active[:, local : local + N]
    readout = active[:, local + N :].astype(bf16)
    steps = jax.nn.softplus(projected[:, local + channels :] + by_head[0:1, :])
    rows = lax.broadcasted_iota(jnp.int32, (width, width), 0)
    cols = lax.broadcasted_iota(jnp.int32, (width, width), 1)
    running = running_sum(steps * by_head[1:2, :])
    across = running.T
    meeting = jnp.where(cols <= rows, dot_nt(readout, entry.astype(bf16)), 0.0)
    before = state[...].astype(bf16)
    states[0] = before
    carried = dot(readout, before)
    entry_t = entry.T.astype(bf16)
    low = lax.broadcasted_iota(jnp.int32, (width, LANES), 1) < HEAD
    total = jnp.zeros((width, LANES), f32)
    weighted, decay = [], []
    for p in range(local // LANES):
        at = slice(p * LANES, (p + 1) * LANES)
        signal = active[:, at]
        mixing, along = [], []
        for h in (2 * p, 2 * p + 1):
            along.append(jnp.broadcast_to(running[:, h : h + 1], (width, width)))
            span = jnp.minimum(along[-1] - across[h : h + 1, :], 0.0)
            mixing.append((jnp.exp(span) * meeting).astype(bf16))
        entered = signal * spread_pair(low, steps, p)
        y = dot(jnp.concatenate(mixing, axis=1), stacked(low, entered))
        along = jnp.where(low, along[0], along[1])
        grown_p = jnp.exp(along)
        y = y + grown_p * carried[:, at] + by_channel[6:7, at] * signal
        result[:, at] = y
        gate = projected[:, at]
        gated = y * gate * sigmoid(gate)
        scaled[:, at] = (gated * by_channel[5:6, at]).astype(bf16)
        total = total + gated * gated
        weighted.append((entered * jnp.exp(along[width - 1 : width, :] - along)).astype(bf16))
        decay.append(grown_p[width - 1 : width, :])
    squares[...] = jnp.sum(total, axis=1, keepdims=True)
    state[...] = jnp.concatenate(decay, axis=1) * state[...] + dot(
        entry_t, jnp.concatenate(weighted, axis=1)
    )


def backward_kernel(
    rank,
    projected,
    tail,
    g_result,
    g_gate,
    states,
    by_channel,
    by_head,
    g_projected,
    sum_channel,
    sum_head,
    adjoint,
    window,
    ahead,
):
    step = pl.program_id(0)
    last = pl.num_programs(0) - 1
    width, local = g_result.shape
    channels = local + 2 * N
    taps = 4

    @pl.when(step == 0)
    def _():
        adjoint[...] = jnp.zeros_like(adjoint)
        ahead[width : width + 8, :] = jnp.zeros((8, channels), f32)
        sum_channel[...] = jnp.zeros_like(sum_channel)
        sum_head[...] = jnp.zeros_like(sum_head)

    @pl.when(step > 0)
    def _():
        ahead[width : width + 8, :] = ahead[0:8, :]

    window[0:8, :] = jnp.where(step == last, 0.0, tail[:, local : local + channels])
    window[8 : 8 + width, :] = projected[:, local : local + channels]
    filtered = by_channel[4:5, :]
    for tap in range(taps):
        at = 9 - taps + tap
        filtered = filtered + by_channel[tap : tap + 1, :] * window[at : at + width, :]
    gate_f = sigmoid(filtered)
    active = filtered * gate_f
    slope = gate_f * (1.0 + filtered * (1.0 - gate_f))
    entry = active[:, local : local + N]
    readout = active[:, local + N :]
    entry_b, readout_b = entry.astype(bf16), readout.astype(bf16)
    shifted = projected[:, local + channels :] + by_head[0:1, :]
    steps = jax.nn.softplus(shifted)
    rate = by_head[1:2, :]
    rows = lax.broadcasted_iota(jnp.int32, (width, width), 0)
    cols = lax.broadcasted_iota(jnp.int32, (width, width), 1)
    falls = steps * rate
    running = running_sum(falls)
    across = running.T
    meeting = jnp.where(rows <= cols, dot_nt(entry_b, readout_b), 0.0)
    before = states[0]
    after = adjoint[...].astype(bf16)
    carried = dot(readout_b, before)
    returned = dot(entry_b, after)
    readout_t = readout.T.astype(bf16)
    lane = lax.broadcasted_iota(jnp.int32, (width, LANES), 1)
    low = lane < HEAD
    g_projected[:, 0:local] = g_gate[...]
    ones = jnp.ones((width, LANES), bf16)
    by_col = jnp.zeros((width, LANES), f32)
    pick_rows = lax.broadcasted_iota(jnp.int32, (LANES, LANES), 0) // HEAD
    pick_cols = lax.broadcasted_iota(jnp.int32, (LANES, LANES), 1)
    g_meeting = jnp.zeros((width, width), f32)
    by_row = []
    per_head = jnp.zeros((3 * width + 8, LANES), f32)
    g_entry = jnp.zeros((width, N), f32)
    g_readout = jnp.zeros((width, N), f32)
    for p in range(local // LANES):
        at = slice(p * LANES, (p + 1) * LANES)
        signal = active[:, at]
        g_y = g_result[:, at].astype(f32)
        steps_p = spread_pair(low, steps, p)
        entered = signal * steps_p
        g_mixing = dot_nt(stacked(low, entered), g_result[:, at])
        mixing, along, parts = [], [], []
        for k, h in enumerate((2 * p, 2 * p + 1)):
            along.append(jnp.broadcast_to(running[:, h : h + 1], (width, width)))
            span = jnp.minimum(across[h : h + 1, :] - along[-1], 0.0)
            kernel = jnp.exp(span)
            mixing.append((kernel * meeting).astype(bf16))
            part = g_mixing[k * width : (k + 1) * width, :] * kernel
            g_meeting = g_meeting + part
            parts.append((part * meeting).astype(bf16))
            by_row.append(jnp.sum(parts[-1].astype(f32), axis=0, keepdims=True))
        across_sum = dot(jnp.concatenate(parts, axis=0), ones)
        for k, h in enumerate((2 * p, 2 * p + 1)):
            by_col = jnp.where(lane == h, across_sum[k * width : (k + 1) * width], by_col)
        along = jnp.where(low, along[0], along[1])
        grown_p = jnp.exp(along)
        left_p = jnp.exp(along[width - 1 : width, :] - along)
        back = left_p * returned[:, at]
        through = dot(jnp.concatenate(mixing, axis=1), stacked(low, g_y)) + back
        skip = by_channel[6:7, at]
        ahead[0:width, at] = steps_p * through + skip * g_y
        sum_channel[5:6, at] += jnp.sum(g_y * signal, axis=0, keepdims=True)
        g_grown = grown_p * g_y
        g_grown_b = g_grown.astype(bf16)
        before_p = before[:, at]
        after_p = adjoint[:, at]
        held = jnp.sum(after_p * before_p.astype(f32), axis=0, keepdims=True)
        pieces = jnp.concatenate(
            [
                signal * through,
                entered * back,
                g_grown * carried[:, at],
                jnp.broadcast_to(held, (8, LANES)),
            ],
            axis=0,
        )
        pick = jnp.where(pick_rows + 2 * p == pick_cols, 1.0, 0.0)
        per_head = per_head + dot(pieces.astype(bf16), pick.astype(bf16))
        g_readout = g_readout + dot_nt(g_grown_b, before_p)
        g_entry = g_entry + dot_nt((left_p * entered).astype(bf16), after[:, at])
        adjoint[:, at] = grown_p[width - 1 : width, :] * after_p + dot(readout_t, g_grown_b)
    g_meeting = jnp.where(rows <= cols, g_meeting, 0.0)
    g_readout = g_readout + dot(g_meeting.T.astype(bf16), entry_b)
    g_entry = g_entry + dot(g_meeting.astype(bf16), readout_b)
    heads = len(by_row)
    by_row = jnp.concatenate(by_row + [jnp.zeros((LANES - heads, width), f32)], axis=0).T
    direct = per_head[0:width]
    entering = per_head[width : 2 * width]
    rising = by_row + per_head[2 * width : 3 * width] - by_col
    change = entering - rising
    g_falls = (
        running_sum(change)
        - change
        + jnp.sum(rising, axis=0, keepdims=True)
        + jnp.exp(running[width - 1 : width, :]) * per_head[3 * width : 3 * width + 1]
    )
    g_steps = rate * g_falls + direct
    g_raw = g_steps * sigmoid(shifted)
    sum_head[0:1, :] += jnp.sum(g_raw, axis=0, keepdims=True)
    sum_head[1:2, :] += jnp.sum(falls * g_falls, axis=0, keepdims=True)
    g_projected[:, local + channels :] = g_raw.astype(bf16)
    ahead[0:width, local : local + N] = g_entry
    ahead[0:width, local + N :] = g_readout
    g_filtered = ahead[0:width, :] * slope
    ahead[0:width, :] = g_filtered
    g_in = jnp.zeros((width, channels), f32)
    for tap in range(taps):
        back_at = taps - 1 - tap
        g_in = g_in + by_channel[tap : tap + 1, :] * ahead[back_at : back_at + width, :]
        at = 9 - taps + tap
        sum_channel[tap : tap + 1, :] += jnp.sum(
            g_filtered * window[at : at + width, :], axis=0, keepdims=True
        )
    sum_channel[4:5, :] += jnp.sum(g_filtered, axis=0, keepdims=True)
    g_projected[:, local : local + channels] = g_in.astype(bf16)


def reversed_bits(chip, count):
    bits = count.bit_length() - 1
    return sum(((chip >> k) & 1) << (bits - 1 - k) for k in range(bits))


def slot_of(place, rank, pieces):
    count = pieces // 2
    half = count // 2
    core = (place ^ rank) & 1
    chip = (place ^ rank) >> 1
    at = jnp.where(core == 0, chip, reversed_bits(chip, count))
    return jnp.where(at < half, count, -half) + core * half + at


def chip_order(turn, count):
    return [j if turn == 0 else reversed_bits(j, count) for j in range(count)]


def slot_order(count):
    half = count // 2
    orders = [chip_order(turn, count) for turn in range(2)]
    return [
        (turn, orders[turn][upper * half + low])
        for upper in (1, 0)
        for turn in range(2)
        for low in range(half)
    ]


def scan_forward(rank, projected, by_channel, by_head, local, width):
    length, columns = projected.shape
    count = length // width
    channels = local + 2 * N

    def here(i, rank):
        return (slot_of(i, rank[0], count), 0)

    def fixed(i, rank):
        return (0, 0)

    return pl.pallas_call(
        forward_kernel,
        grid_spec=pltpu.PrefetchScalarGridSpec(
            num_scalar_prefetch=1,
            grid=(count,),
            in_specs=[
                pl.BlockSpec((width, columns), here),
                pl.BlockSpec((8, channels), fixed),
                pl.BlockSpec((8, LANES), fixed),
            ],
            out_specs=[
                pl.BlockSpec((width, local), here),
                pl.BlockSpec((width, local), here),
                pl.BlockSpec((width, 1), here),
                pl.BlockSpec((1, N, local), lambda i, rank: (i, 0, 0)),
            ],
            scratch_shapes=[
                pltpu.VMEM((N, local), f32),
                pltpu.VMEM((width + 8, channels), f32),
            ],
        ),
        out_shape=[
            jax.ShapeDtypeStruct((length, local), f32),
            jax.ShapeDtypeStruct((length, local), bf16),
            jax.ShapeDtypeStruct((length, 1), f32),
            jax.ShapeDtypeStruct((count, N, local), bf16),
        ],
        compiler_params=pltpu.CompilerParams(vmem_limit_bytes=VMEM),
        cost_estimate=pl.CostEstimate(flops=1_000_000, bytes_accessed=1_000_000, transcendentals=0),
        name="scan_forward",
    )(rank, projected, by_channel, by_head)


def scan_backward(rank, projected, g_result, g_gate, states, by_channel, by_head, width):
    length, columns = projected.shape
    local = g_result.shape[1]
    count = length // width
    channels = local + 2 * N

    def here(i, rank):
        return (slot_of(count - 1 - i, rank[0], count), 0)

    def tail(i, rank):
        earlier = jnp.maximum(count - 2 - i, 0)
        return (slot_of(earlier, rank[0], count) * (width // 8) + (width // 8 - 1), 0)

    def fixed(i, rank):
        return (0, 0)

    return pl.pallas_call(
        backward_kernel,
        grid_spec=pltpu.PrefetchScalarGridSpec(
            num_scalar_prefetch=1,
            grid=(count,),
            in_specs=[
                pl.BlockSpec((width, columns), here),
                pl.BlockSpec((8, columns), tail),
                pl.BlockSpec((width, local), here),
                pl.BlockSpec((width, local), here),
                pl.BlockSpec((1, N, local), lambda i, rank: (count - 1 - i, 0, 0)),
                pl.BlockSpec((8, channels), fixed),
                pl.BlockSpec((8, LANES), fixed),
            ],
            out_specs=[
                pl.BlockSpec((width, columns), here),
                pl.BlockSpec((8, channels), fixed),
                pl.BlockSpec((8, LANES), fixed),
            ],
            scratch_shapes=[
                pltpu.VMEM((N, local), f32),
                pltpu.VMEM((width + 8, channels), f32),
                pltpu.VMEM((width + 8, channels), f32),
            ],
        ),
        out_shape=[
            jax.ShapeDtypeStruct((length, columns), bf16),
            jax.ShapeDtypeStruct((8, channels), f32),
            jax.ShapeDtypeStruct((8, LANES), f32),
        ],
        compiler_params=pltpu.CompilerParams(vmem_limit_bytes=VMEM),
        cost_estimate=pl.CostEstimate(flops=1_000_000, bytes_accessed=1_000_000, transcendentals=0),
        name="scan_backward",
    )(rank, projected, projected, g_result, g_gate, states, by_channel, by_head)


BELOW = 16


def pack_kernel(
    place,
    in_weight,
    step_weight,
    filter_weight,
    filter_bias,
    inner_gain,
    norm_gain,
    per_head,
    *refs,
):
    parts, spread = refs[:-1], refs[-1]
    chips = len(parts)
    rows, columns = in_weight.shape[0], parts[0].shape[1]
    heads = step_weight.shape[1]
    local = (columns - 2 * N - LANES) // 2
    inner = local * chips
    channels = local + 2 * N
    each = heads // chips
    chip, core = place[0], place[1]
    taps, mine = filter_weight.shape
    at_row = lax.broadcasted_iota(jnp.int32, (heads, LANES), 0)
    at_lane = lax.broadcasted_iota(jnp.int32, (heads, LANES), 1)

    def laid(a, width, at):
        a = jnp.pad(a.astype(f32), ((0, 0), (0, width - a.shape[1])))
        return pltpu.roll(a, at, 1)

    filters = jnp.concatenate(
        [
            filter_weight[...].astype(f32),
            filter_bias[...].astype(f32),
            jnp.zeros((8 - taps - 1, mine), f32),
        ],
        axis=0,
    )
    spread[...] = laid(filters, spread.shape[1], (2 * chip + core) * mine)
    gain = laid(norm_gain[...], -(-chips * rows // LANES) * LANES, chip * rows)
    inner_row = laid(inner_gain[...], local, core * inner_gain.shape[1])
    head_rows = laid(per_head[...], LANES, core * (each // 2))
    for j in range(chips):
        c = chip ^ j
        out = parts[j]
        at = pl.ds(0, rows)
        from_gate = pl.ds(pl.multiple_of(c * local, LANES), local)
        out[at, 0:local] = in_weight[:, from_gate]
        out[at, local : 2 * local] = in_weight[
            :, pl.ds(pl.multiple_of(inner + c * local, LANES), local)
        ]
        out[at, 2 * local : 2 * local + 2 * N] = in_weight[:, 2 * inner :]
        pick = jnp.logical_and(at_row == c * each + at_lane, at_lane < each)
        pick = jnp.where(pick, 1.0, 0.0).astype(bf16)
        out[at, 2 * local + 2 * N :] = dot(step_weight[...], pick).astype(bf16)
        top = jnp.concatenate([spread[:, from_gate], spread[:, inner:]], axis=1)
        if j == 0:
            row = lax.broadcasted_iota(jnp.int32, (8, channels), 0)
            wide = jnp.pad(inner_row, ((0, 0), (0, 2 * N)))
            top = jnp.where(row == 5, wide, top)
        low = [jnp.zeros((8, LANES), f32) if j else head_rows, jnp.broadcast_to(gain, (8, gain.shape[1]))]
        low = jnp.concatenate(low, axis=1)
        low = jnp.pad(low, ((0, 0), (0, columns - low.shape[1])))
        top = jnp.pad(top, ((0, 0), (0, columns - channels)))
        out[rows:, :] = jnp.concatenate([top, low], axis=0).astype(bf16)


def pack_columns(place, arrays, per_head, chips, columns, inner):
    rows = arrays[0].shape[0] + BELOW
    vmem = pl.BlockSpec(memory_space=pltpu.VMEM)
    return pl.pallas_call(
        pack_kernel,
        in_specs=[pl.BlockSpec(memory_space=pltpu.SMEM)] + [vmem] * (len(arrays) + 1),
        out_specs=[vmem] * chips,
        out_shape=[jax.ShapeDtypeStruct((rows, columns), bf16)] * chips,
        scratch_shapes=[pltpu.VMEM((8, inner + 2 * N), f32)],
        compiler_params=pltpu.CompilerParams(vmem_limit_bytes=VMEM),
        cost_estimate=pl.CostEstimate(flops=1_000_000, bytes_accessed=1_000_000, transcendentals=0),
        name="pack_columns",
    )(place, *arrays, per_head)


def parameter_kernel(side, *refs):
    parts, (by_channel, by_head, gain) = refs[:-3], refs[-3:]
    channels = by_channel.shape[1]
    half = len(parts) // 2
    sums = [
        sum((part[...].astype(f32) for part in parts[k * half + 1 : (k + 1) * half]), parts[k * half][...].astype(f32))
        for k in range(2)
    ]
    whole = sums[0] + sums[1]
    heads = whole[8:16, 0:LANES]
    head = lax.broadcasted_iota(jnp.int32, (LANES, channels), 0)
    lane = lax.broadcasted_iota(jnp.int32, (LANES, channels), 1)
    expand = jnp.where(head == lane // HEAD, 1.0, 0.0).astype(bf16)
    skip = dot(heads[2:3].astype(bf16), expand)
    row = lax.broadcasted_iota(jnp.int32, (8, channels), 0)
    by_channel[...] = jnp.where(row == 6, skip, whole[0:8, 0:channels])
    row = lax.broadcasted_iota(jnp.int32, (8, LANES), 0)
    by_head[...] = jnp.where(
        row == 0, heads, jnp.where(row == 1, -jnp.exp(heads), 0.0)
    )
    gain[:, 0:side] = sums[0][8:9, LANES : LANES + side]
    gain[:, side:] = sums[1][8:9, LANES : LANES + side]


def parameters(parts, channels, width):
    total, columns = parts[0].shape
    at = total // BELOW - 1

    def whole(shape):
        return pl.BlockSpec(shape, lambda i: (0, 0))

    shapes = [(8, channels), (8, LANES), (1, width)]
    return pl.pallas_call(
        lambda *refs: parameter_kernel(width // 2, *refs),
        grid=(1,),
        in_specs=[pl.BlockSpec((BELOW, columns), lambda i: (at, 0))] * len(parts),
        out_specs=[whole(shape) for shape in shapes],
        out_shape=[jax.ShapeDtypeStruct(shape, f32) for shape in shapes],
        compiler_params=pltpu.CompilerParams(vmem_limit_bytes=VMEM),
        cost_estimate=pl.CostEstimate(flops=1_000_000, bytes_accessed=1_000_000, transcendentals=0),
        name="parameters",
    )(*parts)


def assemble_kernel(place, *refs):
    parts, out = refs[:-1], refs[-1]
    chips = len(parts) // 2
    rows = parts[0].shape[0] - BELOW
    for k in range(2):
        for j in range(chips):
            at = pl.multiple_of((k * chips + (place[0] ^ j)) * rows, BELOW)
            out[pl.ds(at, rows), :] = parts[k * chips + j][0:rows, :]


def assembled(place, parts):
    vmem = pl.BlockSpec(memory_space=pltpu.VMEM)
    rows, columns = parts[0].shape
    return pl.pallas_call(
        assemble_kernel,
        in_specs=[pl.BlockSpec(memory_space=pltpu.SMEM)] + [vmem] * len(parts),
        out_specs=vmem,
        out_shape=jax.ShapeDtypeStruct(((rows - BELOW) * len(parts), columns), bf16),
        compiler_params=pltpu.CompilerParams(vmem_limit_bytes=VMEM),
        cost_estimate=pl.CostEstimate(flops=1_000_000, bytes_accessed=1_000_000, transcendentals=0),
        name="assembled",
    )(place, *parts)


def split_kernel(ranks, core, tokens, mine, sent):
    batch, piece, width = tokens.shape
    half = batch // 2
    rows = width // ranks
    first = core[0] == 0
    for b in range(batch):
        parts = [
            jnp.concatenate(
                [
                    tokens[b, :, c * rows : (c + 1) * rows].astype(f32)
                    for c in range(k, ranks, 2)
                ],
                axis=1,
            )
            for k in range(2)
        ]
        own = jnp.where(first, parts[0], parts[1])
        other = jnp.where(first, parts[1], parts[0])
        here = first if b < half else jnp.logical_not(first)

        @pl.when(here)
        def _():
            mine[b % half] = jnp.concatenate([own, other], axis=1).astype(bf16)

        @pl.when(jnp.logical_not(here))
        def _():
            sent[b % half] = jnp.concatenate([other, own], axis=1).astype(bf16)


def split_tokens(core, tokens, ranks):
    batch, piece, width = tokens.shape
    vmem = pl.BlockSpec(memory_space=pltpu.VMEM)
    shape = jax.ShapeDtypeStruct((batch // 2, piece, width), bf16)
    return pl.pallas_call(
        lambda *refs: split_kernel(ranks, *refs),
        in_specs=[pl.BlockSpec(memory_space=pltpu.SMEM), vmem],
        out_specs=[vmem, vmem],
        out_shape=[shape, shape],
        compiler_params=pltpu.CompilerParams(vmem_limit_bytes=VMEM),
        cost_estimate=pl.CostEstimate(flops=1_000_000, bytes_accessed=1_000_000, transcendentals=0),
        name="split_tokens",
    )(core, tokens)


def distinct(pieces):
    arrays, where = [], []
    for array, index in pieces:
        found = [k for k, a in enumerate(arrays) if a is array]
        if not found:
            arrays.append(array)
            found = [len(arrays) - 1]
        where.append((found[0], index))
    return arrays, where


def rows_call(kernel, pieces, extra, name):
    arrays, where = distinct(pieces)
    vmem = pl.BlockSpec(memory_space=pltpu.VMEM)
    rows, width = arrays[0].shape[1:]
    return pl.pallas_call(
        lambda *refs: kernel(where, *refs),
        in_specs=[vmem] * (len(arrays) + len(extra)),
        out_specs=vmem,
        out_shape=jax.ShapeDtypeStruct((rows * len(where), width), bf16),
        compiler_params=pltpu.CompilerParams(vmem_limit_bytes=VMEM),
        cost_estimate=pl.CostEstimate(flops=1_000_000, bytes_accessed=1_000_000, transcendentals=0),
        name=name,
    )(*extra, *arrays)


def project_kernel(where, gain, columns, *refs):
    pieces, (out, projected) = refs[:-2], refs[-2:]
    rows = pieces[0].shape[1]

    @pl.when(pl.program_id(0) == 0)
    def _():
        for k, (a, index) in enumerate(where):
            values = pieces[a][index].astype(f32)
            scale = lax.rsqrt(jnp.mean(values * values, axis=1, keepdims=True) + EPSILON)
            out[k * rows : (k + 1) * rows, :] = (values * scale * gain[...]).astype(bf16)

    tile = 256
    for k in range(out.shape[0] // tile):
        at = slice(k * tile, (k + 1) * tile)
        projected[at, :] = dot(out[at, :], columns[...])


def project(pieces, gain, columns):
    arrays, where = distinct(pieces)
    rows, width = arrays[0].shape[1:]
    length, wide = rows * len(where), columns.shape[1]
    tile = 384 if wide % 384 == 0 else LANES

    def whole(shape):
        return pl.BlockSpec(shape, lambda i: (0,) * len(shape))

    return pl.pallas_call(
        lambda *refs: project_kernel(where, *refs),
        grid=(wide // tile,),
        in_specs=[whole(gain.shape), pl.BlockSpec((width, tile), lambda i: (0, i))]
        + [whole(a.shape) for a in arrays],
        out_specs=[whole((length, width)), pl.BlockSpec((length, tile), lambda i: (0, i))],
        out_shape=[
            jax.ShapeDtypeStruct((length, width), bf16),
            jax.ShapeDtypeStruct((length, wide), f32),
        ],
        compiler_params=pltpu.CompilerParams(vmem_limit_bytes=VMEM),
        cost_estimate=pl.CostEstimate(flops=1_000_000, bytes_accessed=1_000_000, transcendentals=0),
        name="project",
    )(gain, columns, *arrays)


def joined_kernel(where, *refs):
    pieces, out = refs[:-1], refs[-1]
    rows = pieces[0].shape[1]
    for k, (a, index) in enumerate(where):
        out[k * rows : (k + 1) * rows, :] = pieces[a][index]


def joined_rows(pieces):
    return rows_call(joined_kernel, pieces, [], "joined_rows")


def gate_kernel(result, projected, g_mixed, norms, by_channel, g_result, g_gate, mixed):
    local = result.shape[1]
    gain = by_channel[5:6, 0:local]
    r = norms[:, 0:1]
    y = result[...]
    gate = projected[...]
    gate_s = sigmoid(gate)
    silu = gate * gate_s
    gated = y * silu
    mixed[...] = (gated * r * gain).astype(bf16)
    g_gated = r * gain * g_mixed[...] - gated * norms[:, 1:2]
    g_result[...] = (g_gated * silu).astype(bf16)
    g_gate[...] = (g_gated * y * gate_s * (1.0 + gate * (1.0 - gate_s))).astype(bf16)


def gate_gradients(result, projected, g_mixed, norms, by_channel):
    length, local = result.shape
    width = 256

    def here(i):
        return (i, 0)

    block = pl.BlockSpec((width, local), here)
    return pl.pallas_call(
        gate_kernel,
        grid=(length // width,),
        in_specs=[
            block,
            block,
            block,
            pl.BlockSpec((width, 2), here),
            pl.BlockSpec(by_channel.shape, lambda i: (0, 0)),
        ],
        out_specs=[block] * 3,
        out_shape=[jax.ShapeDtypeStruct((length, local), bf16)] * 3,
        compiler_params=pltpu.CompilerParams(vmem_limit_bytes=VMEM),
        cost_estimate=pl.CostEstimate(flops=1_000_000, bytes_accessed=1_000_000, transcendentals=0),
        name="gate_gradients",
    )(result, projected, g_mixed, norms, by_channel)


def output_kernel(core, tokens, kept, got, output):
    batch = tokens.shape[0]
    half = batch // 2
    for b in range(batch):
        mine = core[0] == b // half
        total = jnp.where(mine, kept[b % half], got[b % half].astype(f32))
        output[b] = (tokens[b].astype(f32) + total).astype(bf16)


def token_kernel(ranks, core, tokens, cotangent, gain, kept, got, gradient):
    batch, _, width = tokens.shape
    half, side, rows = batch // 2, width // 2, width // ranks
    gains = (gain[:, :side], gain[:, side:])
    first = core[0] == 0
    gains = (jnp.where(first, gains[0], gains[1]), jnp.where(first, gains[1], gains[0]))
    for b in range(batch):
        owner = b // half
        g = jnp.where(core[0] == owner, kept[b % half], got[b % half].astype(f32))
        parts = (g[:, :side], g[:, side:]) if owner == 0 else (g[:, side:], g[:, :side])
        parts = (parts[0] * gains[0], parts[1] * gains[1])
        weighted = jnp.concatenate(
            [part[:, c * rows : (c + 1) * rows] for c in range(ranks // 2) for part in parts],
            axis=1,
        )
        values = tokens[b].astype(f32)
        scale = lax.rsqrt(jnp.mean(values * values, axis=1, keepdims=True) + EPSILON)
        inner = jnp.mean(values * weighted, axis=1, keepdims=True)
        gradient[b] = (
            cotangent[b].astype(f32) + scale * weighted - values * (scale * scale * scale * inner)
        )


def share_kernel(chips, place, summed, *parts):
    share, columns = parts[0].shape
    width = summed.shape[1]
    for j in range(chips):
        c = place[0] ^ j
        for k in range(columns // width):
            at = pl.multiple_of((k * chips + c) * share, share)
            parts[j][:, k * width : (k + 1) * width] = summed[pl.ds(at, share), :]


def shares_by_chip(place, summed, chips, share, columns):
    vmem = pl.BlockSpec(memory_space=pltpu.VMEM)
    return pl.pallas_call(
        lambda *refs: share_kernel(chips, *refs),
        in_specs=[pl.BlockSpec(memory_space=pltpu.SMEM), vmem],
        out_specs=[vmem] * chips,
        out_shape=[jax.ShapeDtypeStruct((share, columns), bf16)] * chips,
        compiler_params=pltpu.CompilerParams(vmem_limit_bytes=VMEM),
        cost_estimate=pl.CostEstimate(flops=1_000_000, bytes_accessed=1_000_000, transcendentals=0),
        name="shares_by_chip",
    )(place, summed)


def early_kernel(across, place, summed, *refs):
    parts, out = refs[:-1], refs[-1]
    share, local = parts[0].shape
    chips = len(parts)
    inner = chips * local
    for j, part in enumerate(parts):
        out[:, pl.ds(pl.multiple_of((place[0] ^ j) * local, LANES), local)] = part[...]
    rounds = (summed.shape[0] // share - chips) // across
    for k in range(across):
        for r in range(rounds):
            start = chips * share + (k * rounds + r) * share
            to = inner + (r * across + k) * local
            out[:, to : to + local] = summed[start : start + share, :]


def late_kernel(heads, place, *refs):
    parts, out = refs[:-1], refs[-1]
    chips = len(parts)
    each = heads // chips
    columns = parts[0].shape[1]
    local = columns - 2 * N - LANES
    inner = chips * local
    row = lax.broadcasted_iota(jnp.int32, (LANES, heads), 0)
    lane = lax.broadcasted_iota(jnp.int32, (LANES, heads), 1)
    steps = jnp.zeros((out.shape[0], heads), f32)
    shared = jnp.zeros((out.shape[0], 2 * N), f32)
    for j, part in enumerate(parts):
        c = place[0] ^ j
        out[:, pl.ds(pl.multiple_of(c * local, LANES), local)] = part[:, 0:local]
        shared = shared + part[:, local : local + 2 * N].astype(f32)
        pick = jnp.logical_and(lane == c * each + row, row < each)
        steps = steps + dot(part[:, local + 2 * N :], jnp.where(pick, 1.0, 0.0).astype(bf16))
    out[:, inner : inner + 2 * N] = shared.astype(bf16)
    out[:, inner + 2 * N :] = steps.astype(bf16)


def joined_shares(kernel, place, arrays, shape, name):
    vmem = pl.BlockSpec(memory_space=pltpu.VMEM)
    return pl.pallas_call(
        kernel,
        in_specs=[pl.BlockSpec(memory_space=pltpu.SMEM)] + [vmem] * len(arrays),
        out_specs=vmem,
        out_shape=jax.ShapeDtypeStruct(shape, bf16),
        compiler_params=pltpu.CompilerParams(vmem_limit_bytes=VMEM),
        cost_estimate=pl.CostEstimate(flops=1_000_000, bytes_accessed=1_000_000, transcendentals=0),
        name=name,
    )(place, *arrays)


def weights_kernel(early, rest, in_weight, step_weight, total_in, total_step, by_gain):
    inner = in_weight.shape[1] - 2 * N - early_columns(in_weight)
    heads = step_weight.shape[1]
    first = early[:, 0:inner].astype(f32)
    last = rest[:, 0 : inner + 2 * N].astype(f32)
    step = rest[:, inner + 2 * N :].astype(f32)
    total_in[:, 0:inner] = first
    total_in[:, inner:] = last
    total_step[...] = step
    by_gain[...] = (
        jnp.sum(in_weight[:, 0:inner].astype(f32) * first, axis=1, keepdims=True)
        + jnp.sum(in_weight[:, inner:].astype(f32) * last, axis=1, keepdims=True)
        + jnp.sum(step_weight[...].astype(f32) * step, axis=1, keepdims=True)
    )


def early_columns(in_weight):
    return (in_weight.shape[1] - 2 * N) // 2


def weight_totals(early, rest, in_weight, step_weight):
    rows = in_weight.shape[0]
    block = rows // 4 if rows % 64 == 0 else rows

    def here(i):
        return (i, 0)

    arrays = [early, rest, in_weight, step_weight]
    widths = [in_weight.shape[1], step_weight.shape[1], 1]
    return pl.pallas_call(
        weights_kernel,
        grid=(rows // block,),
        in_specs=[pl.BlockSpec((block, a.shape[1]), here) for a in arrays],
        out_specs=[pl.BlockSpec((block, width), here) for width in widths],
        out_shape=[jax.ShapeDtypeStruct((rows, width), f32) for width in widths],
        compiler_params=pltpu.CompilerParams(vmem_limit_bytes=VMEM),
        cost_estimate=pl.CostEstimate(flops=1_000_000, bytes_accessed=1_000_000, transcendentals=0),
        name="weight_totals",
    )(*arrays)


def whole_call(kernel, scalar, arrays, shape, dtype, name):
    vmem = pl.BlockSpec(memory_space=pltpu.VMEM)
    return pl.pallas_call(
        kernel,
        in_specs=[pl.BlockSpec(memory_space=pltpu.SMEM)] + [vmem] * len(arrays),
        out_specs=vmem,
        out_shape=jax.ShapeDtypeStruct(shape, dtype),
        compiler_params=pltpu.CompilerParams(vmem_limit_bytes=VMEM),
        cost_estimate=pl.CostEstimate(flops=1_000_000, bytes_accessed=1_000_000, transcendentals=0),
        name=name,
    )(scalar, *arrays)


def across_chips(x, bit):
    return lax.ppermute(x, "chip", [(i, i ^ bit) for i in range(lax.axis_size("chip"))])


def sibling(x):
    return lax.ppermute(x, "core", [(0, 1), (1, 0)])


def chip_bits(turn):
    chips = lax.axis_size("chip")
    bits = [1 << k for k in range(chips.bit_length() - 1)]
    return bits if turn == 0 else bits[::-1]


def after(x, *deps):
    return lax.optimization_barrier((x, deps))[0]


class Gather:
    def __init__(self, block):
        self.own = {bit: across_chips(block, bit) for bit in chip_bits(0)}
        self.have = []
        for turn in range(2):
            have = {0: (block, turn)}
            for bit in chip_bits(turn)[:1]:
                have[bit] = (self.own[bit], turn)
            self.have.append(have)

    def received(self):
        return list(self.own.values())

    def relay(self, *deps):
        relayed = []
        for turn, have in enumerate(self.have):
            for bit in chip_bits(turn)[1:]:
                new = {bit: (self.own[bit], turn)}
                for j, (array, index) in sorted(have.items()):
                    if j:
                        part = array[index : index + 1]
                        part = after(part, *deps) if deps else part
                        relayed.append(part)
                        new[j ^ bit] = (across_chips(part, bit), 0)
                have.update(new)
        return relayed

    def slots(self):
        return [self.have[turn][j] for turn, j in slot_order(len(self.have[0]))]


class Scatter:
    def __init__(self, rows, chips, *deps, keep_rows=None):
        self.rows = keep_rows or rows
        self.bits = [chip_bits(turn)[::-1] for turn in range(2)]
        gives = tuple(part.astype(bf16) for part in rows(True))
        self.gives = after(gives, *deps) if deps else gives
        self.kept = None
        self.sent = [across_chips(x, bits[0]) for x, bits in zip(self.gives, self.bits)]

    def step(self, *deps):
        kept = self.rows(False) if self.kept is None else self.kept
        sent = after(tuple(self.sent), *deps) if deps else self.sent
        self.kept, self.sent = [], []
        for turn, bits in enumerate(self.bits):
            bits.pop(0)
            total = kept[turn].astype(f32) + sent[turn].astype(f32)
            if bits:
                half = total.shape[0] // 2
                self.kept.append(total[:half])
                self.sent.append(across_chips(total[half:].astype(bf16), bits[0]))
            else:
                self.kept.append(total)

    def done(self, *deps):
        while self.bits[0]:
            self.step(*deps)
        return [part[0] for part in self.kept]


def chip_total(x):
    order = slot_order(x.shape[-2] // 2)
    for bit in chip_bits(0):
        moved = [order.index((turn, j ^ bit)) for turn, j in order]
        pick = jnp.asarray([[float(m == k) for k in range(len(order))] for m in moved], f32)
        x = x + jnp.einsum("st,atp->asp", pick, across_chips(x, bit), precision=precise)
    return x


def across_groups(x, step):
    return lax.ppermute(x, "dp", [(i, i ^ step) for i in range(lax.axis_size("dp"))])


def by_group(x):
    blocks, rows, width = x.shape
    count = lax.axis_size("dp")
    return x.reshape(blocks, count, rows // count, width).transpose(1, 0, 2, 3)


def group_scatter(x):
    return lax.psum_scatter(x, "dp", scatter_dimension=0, tiled=False)


def group_gather(x):
    return lax.all_gather(x, "dp", axis=0, tiled=True)


def body(
    tokens,
    norm_gain,
    in_weight,
    step_weight,
    filter_weight,
    filter_bias,
    step_bias,
    log_rate,
    skip_scale,
    inner_gain,
    out_weight,
    cotangent,
):
    chips = lax.axis_size("chip")
    chip, core = lax.axis_index("chip"), lax.axis_index("core")
    rank = chip * 2 + core
    batch, piece, width = tokens.shape
    half = batch // 2
    ranks = chips * 2
    heads = log_rate.shape[0] * ranks
    inner = inner_gain.shape[0] * ranks
    local_heads, local = heads // chips, inner // chips
    rows = in_weight.shape[0]
    side = width // 2
    taps = filter_weight.shape[0]
    channels = local + 2 * N
    first = core == 0

    def own_first(a, b):
        return (jnp.where(first, a, b), jnp.where(first, b, a))

    columns_in = 2 * local + 2 * N + LANES
    place = jnp.stack([chip, core]).astype(jnp.int32)
    per_head = jnp.stack([step_bias, log_rate, skip_scale])
    per_head = jnp.pad(per_head, ((0, 5), (0, 0)))
    packed_weight = pack_columns(
        place,
        [
            in_weight,
            step_weight,
            filter_weight,
            filter_bias[None],
            inner_gain[None],
            norm_gain[None],
        ],
        per_head,
        chips,
        columns_in,
        inner,
    )

    def of_core(a, which):
        return lax.dynamic_slice_in_dim(a, which * half, half, 0)

    core_ref = core.astype(jnp.int32).reshape(1)
    mine, sent = split_tokens(after(core_ref, *packed_weight), tokens, ranks)
    got = sibling(sent)
    token_blocks = [jnp.stack([mine[b], got[b]]) for b in range(half)]
    mine_cot, got_cot = of_core(cotangent, core), sibling(of_core(cotangent, 1 - core))
    cot_blocks = [jnp.stack([mine_cot[b], got_cot[b]]) for b in range(half)]

    parts = [across_chips(part, j) if j else part for j, part in enumerate(packed_weight)]
    parts = parts + [sibling(part) for part in parts]
    by_channel, by_head, gain = parameters(parts, channels, width)
    columns = assembled(place, parts)
    out_low, out_high = own_first(out_weight, sibling(out_weight))
    out_rows = jnp.concatenate([out_low, out_high], axis=0)

    def tn(a, b):
        return lax.dot_general(a, b, (((0,), (0,)), ((), ())), preferred_element_type=f32)

    rank_ref = rank.astype(jnp.int32).reshape(1)
    spans = range(half)
    queue = [Gather(token_blocks[0])]
    for block in token_blocks[1:] + cot_blocks:
        queue.append((block, None))
    moved = 0

    def advance(*deps):
        nonlocal moved
        if moved >= len(queue):
            return []
        now = queue[moved]
        before = [part for part, _ in queue[moved - 1].slots()] if moved else []
        relayed = now.relay(*deps, *before)
        moved += 1
        if moved < len(queue):
            waits = now.received() if moved > 1 else [part for part, _ in now.slots()]
            block = after(queue[moved][0], *waits, *deps)
            queue[moved] = Gather(block)
            relayed = relayed + [block]
        return relayed

    def slot_rows(a, run):
        count = a.shape[0] // 2

        def rows(upper):
            part = run(a[:count] if upper else a[count:])
            return part.reshape(2, chips // 2, piece, width)

        return rows

    advance()
    normed, projected, fronts = [], [], []
    for b in spans:
        ready = after(gain, fronts[b - 1][2]) if b else gain
        normed_b, projected_b = project(queue[b].slots(), ready, columns)
        normed.append(normed_b)
        projected.append(projected_b)
        issued = advance(*([projected[0]] if b == 0 else []))
        fronts.append(
            scan_forward(
                rank_ref, projected[b], by_channel, after(by_head, *issued), local, piece
            )
        )
        if b + 1 < half:
            advance(fronts[b][2])
    while moved < len(queue):
        advance(fronts[-1][2])
    cots = queue[half:]

    all_cot, g_mixed, stats = [], [], []
    for b in spans:
        result, scaled, squares, states = fronts[b]
        all_cot.append(joined_rows(cots[b].slots()))
        g_mixed.append(dot_nt(all_cot[b], out_rows))
        both = jnp.stack([squares[:, 0], jnp.sum(scaled.astype(f32) * g_mixed[b], axis=1)])
        stats.append(chip_total(both.reshape(2, ranks, piece)).reshape(both.shape) / inner)
    g_results, g_gates, mixed, outs = [], [], [], []
    for b in spans:
        r = lax.rsqrt(stats[b][0] + EPSILON)
        norms = jnp.stack([r, r * r * r * stats[b][1]], axis=1)
        if b + 1 < half:
            norms = after(norms, *cots[b + 1].received())
        g_result, g_gate, mixed_b = gate_gradients(
            fronts[b][0], projected[b], g_mixed[b], norms, by_channel
        )
        g_results.append(g_result)
        g_gates.append(g_gate)
        mixed.append(mixed_b)
        outs.append(Scatter(slot_rows(mixed_b, lambda x: dot(x, out_rows)), chips))

    def row_sums(parts):
        far = [tn(normed[b][:, side:], parts[b]) for b in range(len(parts))]
        near = [tn(normed[b][:, :side], parts[b]) for b in range(len(parts))]
        return far, near

    def core_sum(far, near, *deps):
        sent = after(sum(far).astype(bf16), *deps)
        total = (sum(near) + sibling(sent).astype(f32)).astype(bf16)
        return total.reshape(chips, rows, -1)

    def by_chip(near):
        found = []
        for j in range(chips):
            part = lax.dynamic_index_in_dim(near, chip ^ j, 0, keepdims=True)
            found.append(across_chips(part, j) if j else part)
        return found

    def exchanged(parts):
        return [across_chips(part, j) if j else part for j, part in enumerate(parts)]

    def in_place(parts, size, total):
        whole = jnp.zeros(parts[0].shape[:2] + (total,), bf16)
        for j, part in enumerate(parts):
            whole = lax.dynamic_update_slice_in_dim(whole, part[:, :, :size], (chip ^ j) * size, 2)
        return whole

    gate_near = core_sum(*row_sums(g_gates))
    out_gradient = sum(tn(mixed[b], all_cot[b]) for b in spans)
    out_near, out_far = own_first(out_gradient[: local // 2], out_gradient[local // 2 :])
    out_near = (out_near + sibling(out_far.astype(bf16)).astype(f32)).astype(bf16)
    groups = lax.axis_size("dp")
    share = rows // groups
    out_near = out_near.reshape(groups, -1, width)
    out_near = jnp.concatenate(
        [out_near[:, :, k : k + local] for k in range(0, width, local)], axis=1
    )
    gate_near = by_group(gate_near).reshape(groups, -1, local)
    early = group_scatter(jnp.concatenate([gate_near, out_near], axis=1))

    g_columns, sums, g_normed, far, near = [], [], [], [], []
    ready = after(by_head, gate_near, out_near, *[x for out in outs for x in out.gives])
    for b in spans:
        g_proj, sum_channel, sum_head = scan_backward(
            rank_ref, projected[b], g_results[b], g_gates[b], fronts[b][3], by_channel, ready, piece
        )
        if b == half - 1:
            g_proj, sum_channel, sum_head = after((g_proj, sum_channel, sum_head), early)
        g_columns.append(g_proj)
        sums.append((sum_channel, sum_head))
        waits = [sum_head]
        for part in outs if b == 0 else g_normed[:b]:
            part.step(sum_head)
        rest = g_proj[:, local:]
        far.append(tn(normed[b][:, side:], rest))
        near.append(tn(normed[b][:, :side], rest))
        if b == 0:
            early = after(early, sum_head)
        if b == half - 1:
            rest_near = core_sum(far, near)
        send = slot_rows(g_proj, lambda x: dot_nt(x, columns))
        late = after(g_proj, rest_near) if b == half - 1 else g_proj
        keep = slot_rows(late, lambda x: dot_nt(x, columns))
        g_normed.append(Scatter(send, chips, *([early] if b == 0 else []), keep_rows=keep))
        if b == 0:
            if share % 16 == 0:
                gate_parts = exchanged(shares_by_chip(place, early, chips, share, local))
                early = joined_shares(
                    lambda *refs: early_kernel(width // local, *refs),
                    place,
                    [early, *gate_parts],
                    (share, 2 * inner),
                    "early_share",
                )
            else:
                gate_parts = by_chip(early[: chips * share].reshape(chips, share, local))
                out_share = jnp.split(early[chips * share :], width // local)
                out_share = jnp.concatenate(out_share, axis=1)
                early = [in_place(gate_parts, local, inner)[0]]
                early = early + jnp.split(out_share, inner // width)
                early = jnp.concatenate(early, axis=1)
            out_sums = [out.done() for out in outs]
            waits = [early] + [x for part in out_sums for x in part]
            early = group_gather(early)
        ready = after(by_head, far[b], near[b], *g_normed[b].gives, *waits)
    early = after(early, rest_near)
    total_out = early[:, inner:].reshape(groups, share, -1, width)
    total_out = total_out.transpose(0, 2, 1, 3).reshape(-1, width)
    late_columns = 2 * N + LANES
    rest_blocks = by_group(rest_near).reshape(groups, -1, local + late_columns)
    if local % late_columns == 0:
        cuts = range(0, local + late_columns, late_columns)
        rest_blocks = [rest_blocks[:, :, k : k + late_columns] for k in cuts]
        rest_sum = group_scatter(jnp.concatenate(rest_blocks, axis=1))
    else:
        cuts = [0]
        rest_sum = group_scatter(rest_blocks)
    if share % 16 == 0:
        rest_parts = shares_by_chip(place, rest_sum, chips, share, local + late_columns)
        rest_total = joined_shares(
            lambda *refs: late_kernel(heads, *refs),
            place,
            exchanged(rest_parts),
            (share, inner + 2 * N + heads),
            "late_share",
        )
    else:
        rest_sum = jnp.concatenate(jnp.split(rest_sum, len(cuts)), axis=1)
        rest_parts = by_chip(rest_sum.reshape(chips, share, -1))
        shared = sum(part[:, :, local : local + 2 * N].astype(f32) for part in rest_parts)
        step_parts = [part[:, :, local + 2 * N :] for part in rest_parts]
        rest_total = jnp.concatenate(
            [
                in_place(rest_parts, local, inner),
                shared.astype(bf16),
                in_place(step_parts, local_heads, heads),
            ],
            axis=2,
        )[0]
    rest_total = group_gather(rest_total)
    total_out = total_out.astype(f32)

    total_in, total_step, total_gain = weight_totals(early, rest_total, in_weight, step_weight)
    total_gain = total_gain[:, 0] / norm_gain.astype(f32)
    total_inner = jnp.sum(out_weight.astype(f32) * total_out, axis=1) / inner_gain.astype(f32)

    def regrouped(parts):
        kept = jnp.stack([part[0] for part in parts])
        got = sibling(jnp.stack([part[1] for part in parts]).astype(bf16))
        return (kept, got)

    g_normed = [part.done(rest_near) for part in g_normed]

    sum_channel = sum(part[0] for part in sums)
    sum_head = sum(part[1] for part in sums)

    def placed(a, size):
        empty = jnp.zeros((a.shape[0], size), f32)
        return lax.dynamic_update_slice_in_dim(empty, a, chip * a.shape[1], 1)

    skip = jnp.sum(sum_channel[5, :local].reshape(local_heads, HEAD), axis=1)[None]
    packed = jnp.concatenate(
        [
            jnp.concatenate(
                [placed(sum_channel[: taps + 1, :local], inner), sum_channel[: taps + 1, local:]],
                axis=1,
            ).reshape(-1),
            placed(jnp.concatenate([sum_head[:2, :local_heads], skip], axis=0), heads).reshape(-1),
        ]
    )
    packed = jnp.pad(packed, (0, -packed.shape[0] % 1024)).reshape(-1, LANES)
    packed = after(packed, rest_near)
    packed = packed + sibling(packed)
    for bit in chip_bits(0):
        packed = packed + across_chips(packed, bit)
    for bit in [1 << k for k in range(lax.axis_size("dp").bit_length() - 1)]:
        packed = packed + across_groups(packed, bit)
    packed = packed.reshape(-1)
    cut = (taps + 1) * (inner + 2 * N)

    def own_of(a):
        size = a.shape[1] // ranks
        return lax.dynamic_slice_in_dim(a, rank * size, size, 1)

    channel_totals = own_of(packed[:cut].reshape(taps + 1, -1))
    head_totals = own_of(packed[cut : cut + 3 * heads].reshape(3, heads))

    kept, got = regrouped(out_sums)
    output = whole_call(output_kernel, core_ref, [tokens, kept, got], tokens.shape, bf16, "output")
    kept, got = regrouped(g_normed)
    token_gradient = whole_call(
        lambda *refs: token_kernel(ranks, *refs),
        core_ref,
        [tokens, cotangent, gain, kept, got],
        tokens.shape,
        f32,
        "token_gradient",
    )
    return (
        output,
        token_gradient,
        total_gain,
        total_in,
        total_step,
        channel_totals[:taps],
        channel_totals[taps],
        head_totals[0],
        head_totals[1],
        head_totals[2],
        total_inner,
        total_out,
    )


def solution(mesh):
    ranks, groups = mesh.shape["sp"], mesh.shape["dp"]
    fine = Mesh(mesh.devices.reshape(ranks // 2, 2, groups), ("chip", "core", "dp"))
    sp = ("chip", "core")
    return jax.shard_map(
        body,
        mesh=fine,
        in_specs=(
            P("dp", sp, None),
            P(sp),
            P(sp, None),
            P(sp, None),
            P(None, sp),
            P(sp),
            P(sp),
            P(sp),
            P(sp),
            P(sp),
            P(sp, None),
            P("dp", sp, None),
        ),
        out_specs=(
            P("dp", sp, None),
            P("dp", sp, None),
            P(sp),
            P(sp, None),
            P(sp, None),
            P(None, sp),
            P(sp),
            P(sp),
            P(sp),
            P(sp),
            P(sp),
            P(sp, None),
        ),
        check_vma=False,
    )
```

time: 1570 us -> 545 us (0.35)
  waiting for transfers between devices: 836 us -> 117 us
  matrix products: 279 us -> 69.9 us
  other arithmetic: 230 us -> 43.7 us
  Pallas kernels: 0 us -> 167 us
  blocking collectives: 111 us -> 0 us
  starting transfers between devices: 4.14 us -> 55.5 us
    all_gather x4 -> x2, waiting for transfers between devices: 389 us -> 21.3 us  [group_gather(): return lax.all_gather(x, 'dp', axis=0, tiled=True)]
    psum x1 -> x0, waiting for transfers between devices: 223 us -> none  [body(): lax.psum((part_gain, part_in, part_step, part_filter, part_fbias, part_sb...]
    dot_general x25 -> x24, matrix products: 279 us -> 69.9 us  [the longest x10 31.3 us: tn(): lax.dot_general(a, b, (((0,), (0,)), ((), ())), preferred_element_type=f32)]
    reduce_scatter x2, waiting for transfers between devices: 195 us -> 0.01 us  [group_scatter(): return lax.psum_scatter(x, 'dp', scatter_dimension=0, tiled=False)]
    pallas_call x0 -> x21, Pallas kernels: none -> 167 us  [the longest x2 50.9 us: scan_backward(): pl.pallas_call(backward_kernel, grid_spec=pltpu.PrefetchScalarGridSpec(nu...]
    select_n x16 -> x1, other arithmetic: 137 us -> 2.83 us  [own_first(): return (jnp.where(first, a, b), jnp.where(first, b, a))]
    ppermute x2 -> x62, waiting for transfers between devices: 0.01 us -> 95.6 us  [the longest x47 92.5 us: across_chips(): lax.ppermute(x, 'chip', [(i, i ^ bit) for i in range(lax.axis_size('chip'...]
    ppermute x2 -> x62, starting transfers between devices: 3.77 us -> 55.4 us  [the longest x47 51.9 us: across_chips(): lax.ppermute(x, 'chip', [(i, i ^ bit) for i in range(lax.axis_size('chip'...]
  transfers between devices with their start and end apart: 11 -> 66, of which waited for: 6 -> 20; matrix products, arithmetic and copies ran while one was open for 30% -> 28% of each run, Pallas kernels for 0% -> 27%
where the time goes in v1:
time: 545 us; the launch traced here: 539 us
  Pallas kernels  167 us (31%)
  waiting for transfers between devices  117 us (21%)
  local copies, waits for them, and re-layouts  70.4 us (13%)
  matrix products  69.9 us (13%)
  starting transfers between devices  55.5 us (10%)
  other arithmetic  43.7 us (8%)
  between operations  15.5 us (3%)
    ppermute x47, waiting for transfers between devices, across_chips(): lax.ppermute(x, 'chip', [(i, i ^ bit) for i in range(lax.axis_size('chip'...  92.5 us
    ppermute x47, starting transfers between devices, across_chips(): lax.ppermute(x, 'chip', [(i, i ^ bit) for i in range(lax.axis_size('chip'...  51.9 us
    pallas_call x2, Pallas kernels, scan_backward(): pl.pallas_call(backward_kernel, grid_spec=pltpu.PrefetchScalarGridSpec(nu...  50.9 us
    dot_general x10, matrix products, tn(): lax.dot_general(a, b, (((0,), (0,)), ((), ())), preferred_element_type=f32)  31.3 us
    dot_general x6, matrix products, dot_nt(): lax.dot_general(a, b, (((1,), (1,)), ((), ())), preferred_element_type=f32)  29 us
    pallas_call x2, Pallas kernels, project(): pl.pallas_call(lambda *refs: project_kernel(where, *refs), grid=(wide //...  27.8 us
    pallas_call x2, Pallas kernels, scan_forward(): pl.pallas_call(forward_kernel, grid_spec=pltpu.PrefetchScalarGridSpec(num...  27.5 us
    all_gather x2, waiting for transfers between devices, group_gather(): return lax.all_gather(x, 'dp', axis=0, tiled=True)  21.3 us
  transfers between devices with their start and end apart: 66, of which 20 were waited for; matrix products, arithmetic and copies ran while one was open for 28% of the time, Pallas kernels for 27%

profile of v1, /device:TPU:0, one launch (start us, length us, event | category | flops | bytes accessed | tf_op | source)
XLA Modules:
  0.0 538.5 jit_solution(17199623031772886566)
XLA Ops:
  32.2 11.0 %collective-permute-done.refs_1_ = bf16[208,1920]{1,0:T(8,128)(2,1)} collective-permute-done((bf16[208,1920]{1,0:T(8,128)(2,1)}, bf16[208,1920]{1,0:T(8,128)(2,1)}, u32[]{:S(2)}, u32[]{:S(2)}) %collective-permute-start) | collective-permute-done | bytes 798752 | tf_op jit(solution)/shard_map/ppermute | solution.py:864
  44.1 15.9 %collective-permute-done.9.refs_4_ = bf16[2,128,1536]{2,1,0:T(8,128)(2,1)} collective-permute-done((bf16[2,128,1536]{2,1,0:T(8,128)(2,1)S(1)}, bf16[2,128,1536]{2,1,0:T(8,128)(2,1)}, u32[]{:S(2)}, u32[]{:S(2)}) %collective-permute-start.9) | collective-permute-done | bytes 786464 | tf_op jit(solution)/shard_map/ppermute | solution.py:864
  64.2 17.1 %collective-permute-done.1.refs_2_ = bf16[208,1920]{1,0:T(8,128)(2,1)} collective-permute-done((bf16[208,1920]{1,0:T(8,128)(2,1)}, bf16[208,1920]{1,0:T(8,128)(2,1)}, u32[]{:S(2)}, u32[]{:S(2)}) %collective-permute-start.1) | collective-permute-done | bytes 798752 | tf_op jit(solution)/shard_map/ppermute | solution.py:864
  86.5 5.1 collective-permute-done.10.refs_3_
  98.3 6.0 %assembled.1.refs_1_ = bf16[1536,1920]{1,0:T(8,128)(2,1)} custom-call(s32[2]{0:T(128)} %pad_add_fusion.place.refs_0_, bf16[208,1920]{1,0:T(8,128)(2,1)} %get-tuple-element.93.refs_0_, bf16[208,1920]{1,0:T(8,128)(2,1)} %collective-permute-done.refs_1_, bf16[208,1920]{1,0:T(8,128)(2,1)} %collective-permute-done.1.refs_2_, ...), custom_call_target="tpu_custom_call" | custom-call | flops 1000000 | bytes 1000000 | tf_op jit(solution)/shard_map/assembled/pallas_call | solution.py:530
  106.1 14.0 %project.2 = (bf16[1024,1536]{1,0:T(8,128)(2,1)}, f32[1024,1920]{1,0:T(8,128)}) custom-call(f32[1,1536]{1,0:T(1,128)} %get-tuple-element.121.refs_0_.refs_3_, bf16[1536,1920]{1,0:T(8,128)(2,1)} %assembled.1.refs_1_, bf16[2,128,1536]{2,1,0:T(8,128)(2,1)} %collective-permute-done.8.refs_2_, bf16[1,128,1536]{2,1,0:T(8,128)(2,1)} %collective-permute-done.10.refs_3_, ...), custom_call_target="tpu_custom_call" | custom-call | flops 1000000 | bytes 1000000 | tf_op jit(solution)/shard_map/project/pallas_call | solution.py:637
  126.8 13.6 %scan_forward.2 = (f32[1024,768]{1,0:T(8,128)}, bf16[1024,768]{1,0:T(8,128)(2,1)}, f32[1024,1]{1,0:T(8,128)}, bf16[8,128,768]{2,1,0:T(8,128)(2,1)}) custom-call(s32[1]{0:T(128)} %bitcast.1.rank, f32[1024,1920]{1,0:T(8,128)} %get-tuple-element.101.projected.tail, f32[8,1024]{1,0:T(8,128)} %get-tuple-element.102.by_channel, f32[8,128]{1,0:T(8,128)} %get-tuple-element.148.by_head), custom_call_target="tpu_custom_call" | custom-call | flops 1000000 | bytes 1000000 | tf_op jit(solution)/shard_map/scan_forward/pallas_call | solution.py:305
  141.4 8.3 %collective-permute-done.18.refs_5_ = bf16[1,128,1536]{2,1,0:T(8,128)(2,1)} collective-permute-done((bf16[1,128,1536]{2,1,0:T(8,128)(2,1)}, bf16[1,128,1536]{2,1,0:T(8,128)(2,1)}, u32[]{:S(2)}, u32[]{:S(2)}) %collective-permute-start.18) | collective-permute-done | bytes 393248 | tf_op jit(solution)/shard_map/ppermute | solution.py:864
  166.3 4.6 fusion.52.g_mixed
  180.0 13.8 %project.3 = (bf16[1024,1536]{1,0:T(8,128)(2,1)}, f32[1024,1920]{1,0:T(8,128)}) custom-call(f32[1,1536]{1,0:T(1,128)} %get-tuple-element.121.refs_0_.refs_3_, bf16[1536,1920]{1,0:T(8,128)(2,1)} %assembled.1.refs_1_, bf16[2,128,1536]{2,1,0:T(8,128)(2,1)} %copy-done.32, bf16[1,128,1536]{2,1,0:T(8,128)(2,1)} %collective-permute-done.17.refs_3_, ...), custom_call_target="tpu_custom_call" | custom-call | flops 1000000 | bytes 1000000 | tf_op jit(solution)/shard_map/project/pallas_call | solution.py:637
  197.9 13.9 %scan_forward.3 = (f32[1024,768]{1,0:T(8,128)}, bf16[1024,768]{1,0:T(8,128)(2,1)}, f32[1024,1]{1,0:T(8,128)}, bf16[8,128,768]{2,1,0:T(8,128)(2,1)}) custom-call(s32[1]{0:T(128)} %bitcast.1.rank, f32[1024,1920]{1,0:T(8,128)} %get-tuple-element.123.projected.tail, f32[8,1024]{1,0:T(8,128)} %get-tuple-element.102.by_channel, f32[8,128]{1,0:T(8,128)} %get-tuple-element.148.by_head), custom_call_target="tpu_custom_call" | custom-call | flops 1000000 | bytes 1000000 | tf_op jit(solution)/shard_map/scan_forward/pallas_call | solution.py:305
  214.2 7.3 %gate_gradients.2 = (bf16[1024,768]{1,0:T(8,128)(2,1)}, bf16[1024,768]{1,0:T(8,128)(2,1)}, bf16[1024,768]{1,0:T(8,128)(2,1)}) custom-call(f32[1024,768]{1,0:T(8,128)} %get-tuple-element.109.result, f32[1024,1920]{1,0:T(8,128)} %get-tuple-element.101.projected.tail, f32[1024,768]{1,0:T(8,128)} %copy-done, f32[1024,2]{1,0:T(8,128)} %copy.61.norms, ...), custom_call_target="tpu_custom_call" | custom-call | flops 1000000 | bytes 1000000 | tf_op jit(solution)/shard_map/gate_gradients/pallas_call | solution.py:687
  242.9 10.3 %collective-permute-done.31 = f32[2,8,128]{2,1,0:T(8,128)S(1)} collective-permute-done((f32[2,8,128]{2,1,0:T(8,128)S(1)}, f32[2,8,128]{2,1,0:T(8,128)S(1)}, u32[]{:S(2)}, u32[]{:S(2)}) %collective-permute-start.31) | collective-permute-done | bytes 8224 | tf_op jit(solution)/shard_map/ppermute | solution.py:864
  254.3 7.8 %gate_gradients.3 = (bf16[1024,768]{1,0:T(8,128)(2,1)}, bf16[1024,768]{1,0:T(8,128)(2,1)}, bf16[1024,768]{1,0:T(8,128)(2,1)}) custom-call(f32[1024,768]{1,0:T(8,128)} %get-tuple-element.127.result, f32[1024,1920]{1,0:T(8,128)} %get-tuple-element.123.projected.tail, f32[1024,768]{1,0:T(8,128)} %copy-done.1, f32[1024,2]{1,0:T(8,128)} %copy.64.norms, ...), custom_call_target="tpu_custom_call" | custom-call | flops 1000000 | bytes 1000000 | tf_op jit(solution)/shard_map/gate_gradients/pallas_call | solution.py:687
  292.1 25.3 %scan_backward.2 = (bf16[1024,1920]{1,0:T(8,128)(2,1)}, f32[8,1024]{1,0:T(8,128)}, f32[8,128]{1,0:T(8,128)}) custom-call(s32[1]{0:T(128)} %bitcast.1.rank, f32[1024,1920]{1,0:T(8,128)} %get-tuple-element.101.projected.tail, f32[1024,1920]{1,0:T(8,128)} %get-tuple-element.101.projected.tail, bf16[1024,768]{1,0:T(8,128)(2,1)} %get-tuple-element.117.g_result, ...), custom_call_target="tpu_custom_call" | custom-call | flops 1000000 | bytes 1000000 | tf_op jit(solution)/shard_map/scan_backward/pallas_call | solution.py:354
  324.4 6.3 %convolution_convert_fusion.1 = bf16[512,1536]{1,0:T(8,128)(2,1)S(1)} fusion(bf16[1536,1920]{1,0:T(8,128)(2,1)} %assembled.1.refs_1_, bf16[1024,1920]{1,0:T(8,128)(2,1)S(1)} %copy-done.65), kind=kOutput, calls=%fused_computation.9 | convolution fusion | flops 3020685312 | bytes 9437184 | tf_op jit(solution)/shard_map/dot_general | solution.py:26
  353.4 6.4 %fusion.5 = f32[768,1152]{1,0:T(8,128)} fusion(bf16[1024,1920]{1,0:T(8,128)(2,1)} %get-tuple-element.138, bf16[1024,1536]{1,0:T(8,128)(2,1)} %get-tuple-element.120), kind=kOutput, calls=%fused_computation.21 | convolution fusion | flops 1811939328 | bytes 7471104 | tf_op jit(solution)/shard_map/dot_general | solution.py:1038
  376.7 25.6 %scan_backward.3 = (bf16[1024,1920]{1,0:T(8,128)(2,1)}, f32[8,1024]{1,0:T(8,128)}, f32[8,128]{1,0:T(8,128)}) custom-call(s32[1]{0:T(128)} %bitcast.1.rank, f32[1024,1920]{1,0:T(8,128)} %get-tuple-element.123.projected.tail, f32[1024,1920]{1,0:T(8,128)} %get-tuple-element.123.projected.tail, bf16[1024,768]{1,0:T(8,128)(2,1)} %get-tuple-element.142.g_result, ...), custom_call_target="tpu_custom_call" | custom-call | flops 1000000 | bytes 1000000 | tf_op jit(solution)/shard_map/scan_backward/pallas_call | solution.py:354
  406.6 5.6 %fusion.2 = bf16[768,1152]{1,0:T(8,128)(2,1)S(1)} fusion(f32[768,1152]{1,0:T(8,128)} %fusion.7, bf16[1024,1920]{1,0:T(8,128)(2,1)} %get-tuple-element.157, bf16[1024,1536]{1,0:T(8,128)(2,1)} %get-tuple-element.122), kind=kOutput, calls=%fused_computation.5 | convolution fusion | flops 1813708800 | bytes 9240576 | tf_op jit(solution)/shard_map/dot_general | solution.py:1038
  430.8 6.5 %fusion.10 = f32[512,1536]{1,0:T(8,128)S(1)} fusion(bf16[1536,1920]{1,0:T(8,128)(2,1)} %assembled.1.refs_1_, bf16[1024,1920]{1,0:T(8,128)(2,1)} %get-tuple-element.157), kind=kOutput, calls=%fused_computation.26 | convolution fusion | flops 3019898880 | bytes 11010048 | tf_op jit(solution)/shard_map/dot_general | solution.py:26
  438.9 5.5 %collective-permute-done.49 = bf16[2,128,1536]{2,1,0:T(8,128)(2,1)} collective-permute-done((bf16[2,128,1536]{2,1,0:T(8,128)(2,1)}, bf16[2,128,1536]{2,1,0:T(8,128)(2,1)}, u32[]{:S(2)}, u32[]{:S(2)}) %collective-permute-start.49) | collective-permute-done | bytes 786464 | tf_op jit(solution)/shard_map/ppermute | solution.py:864
  497.3 5.9 %token_gradient.1 = f32[4,128,1536]{2,1,0:T(8,128)} custom-call(s32[1]{0:T(128)} %bitcast.refs_0_.core, bf16[4,128,1536]{2,1,0:T(8,128)(2,1)} %refs_1_.3, bf16[4,128,1536]{2,1,0:T(8,128)(2,1)} %refs_2_.1, f32[1,1536]{1,0:T(1,128)} %get-tuple-element.121.refs_0_.refs_3_, f32[2,128,1536]{2,1,0:T(8,128)} %pad_maximum_fusion.4.refs_4_, ...), custom_call_target="tpu_custom_call" | custom-call | flops 1000000 | bytes 1000000 | tf_op jit(solution)/shard_map/token_gradient/pallas_call | solution.py:852
  503.2 19.6 %all-gather.5.cloned.1.call-done.rest = bf16[192,3376]{1,0:T(8,128)(2,1)} async-done(((bf16[48,3376]{1,0:T(8,128)(2,1)}), bf16[192,3376]{1,0:T(8,128)(2,1)}) %all-gather.5.cloned.1.call-update) | async-done | bytes 1296400 | tf_op jit(solution)/shard_map/all_gather | solution.py:965
  522.8 5.6 %weight_totals.1 = (f32[192,6400]{1,0:T(8,128)}, f32[192,48]{1,0:T(8,128)}, f32[192,1]{1,0:T(8,128)}) custom-call(bf16[192,6144]{1,0:T(8,128)(2,1)} %all-gather.3.cloned.1.call-done.early, bf16[192,3376]{1,0:T(8,128)(2,1)} %all-gather.5.cloned.1.call-done.rest, bf16[192,6400]{1,0:T(8,128)(2,1)} %in_weight.3, bf16[192,48]{1,0:T(8,128)(2,1)} %copy.58.step_weight), custom_call_target="tpu_custom_call" | custom-call | flops 1000000 | bytes 1000000 | tf_op jit(solution)/shard_map/weight_totals/pallas_call | solution.py:838
  (431 shorter events, 261.9 us)
Async XLA Ops:
  7.2 332.9 %reduce-scatter.3.cloned.1.call-start = ((), (), s32[]{:S(2)}) async-start(), calls=%async_computation.2 | async-start | bytes 2949120 | tf_op jit(solution)/shard_map/reduce_scatter | solution.py:961
  27.1 32.9 %collective-permute-start.9 = (bf16[2,128,1536]{2,1,0:T(8,128)(2,1)S(1)}, bf16[2,128,1536]{2,1,0:T(8,128)(2,1)}, u32[]{:S(2)}, u32[]{:S(2)}) collective-permute-start(bf16[2,128,1536]{2,1,0:T(8,128)(2,1)S(1)} %pad_maximum_fusion.5.refs_6_), channel_id=1, source_target_pairs={{0,8},{8,0},{16,24},{24,16},{1,9},{9,1},{17,25},{25,17},{2,10},{10... | collective-permute-start | bytes 2359304 | tf_op jit(solution)/shard_map/ppermute | solution.py:864
  27.7 32.4 %collective-permute-start.8 = (bf16[2,128,1536]{2,1,0:T(8,128)(2,1)S(1)}, bf16[2,128,1536]{2,1,0:T(8,128)(2,1)}, u32[]{:S(2)}, u32[]{:S(2)}) collective-permute-start(bf16[2,128,1536]{2,1,0:T(8,128)(2,1)S(1)} %pad_maximum_fusion.5.refs_6_), channel_id=1, source_target_pairs={{0,16},{8,24},{16,0},{24,8},{1,17},{9,25},{17,1},{25,9},{2,18},{10... | collective-permute-start | bytes 2359304 | tf_op jit(solution)/shard_map/ppermute | solution.py:864
  29.2 52.1 %collective-permute-start.1 = (bf16[208,1920]{1,0:T(8,128)(2,1)}, bf16[208,1920]{1,0:T(8,128)(2,1)}, u32[]{:S(2)}, u32[]{:S(2)}) collective-permute-start(bf16[208,1920]{1,0:T(8,128)(2,1)} %get-tuple-element.95), channel_id=1, source_target_pairs={{0,16},{8,24},{16,0},{24,8},{1,17},{9,25},{17,1},{25,9},{2,18},{10... | collective-permute-start | bytes 2396168 | tf_op jit(solution)/shard_map/ppermute | solution.py:864
  29.7 53.2 %collective-permute-start.2 = (bf16[208,1920]{1,0:T(8,128)(2,1)}, bf16[208,1920]{1,0:T(8,128)(2,1)}, u32[]{:S(2)}, u32[]{:S(2)}) collective-permute-start(bf16[208,1920]{1,0:T(8,128)(2,1)} %get-tuple-element.96), channel_id=1, source_target_pairs={{0,24},{8,16},{16,8},{24,0},{1,25},{9,17},{17,9},{25,1},{2,26},{10... | collective-permute-start | bytes 2396168 | tf_op jit(solution)/shard_map/ppermute | solution.py:864
  43.2 51.4 %collective-permute-start.3 = (bf16[208,1920]{1,0:T(8,128)(2,1)S(1)}, bf16[208,1920]{1,0:T(8,128)(2,1)}, u32[]{:S(2)}, u32[]{:S(2)}) collective-permute-start(bf16[208,1920]{1,0:T(8,128)(2,1)S(1)} %copy-done.27), channel_id=1, source_target_pairs={{0,4},{4,0},{1,5},{5,1},{2,6},{6,2},{3,7},{7,3},{8,12},{12,8},{9,1... | collective-permute-start | bytes 2396168 | tf_op jit(solution)/shard_map/ppermute | solution.py:868
  60.1 33.1 %collective-permute-start.14 = (bf16[2,128,1536]{2,1,0:T(8,128)(2,1)}, bf16[2,128,1536]{2,1,0:T(8,128)(2,1)}, u32[]{:S(2)}, u32[]{:S(2)}) collective-permute-start(bf16[2,128,1536]{2,1,0:T(8,128)(2,1)} %constant_dynamic-slice_fusion.3), channel_id=1, source_target_pairs={{0,4},{4,0},{1,5},{5,1},{2,6},{6,2},{3,7},{7,3},{8,12},{12,8},{9,1... | collective-permute-start | bytes 2359304 | tf_op jit(solution)/shard_map/ppermute | solution.py:868
  60.1 36.2 %collective-permute-start.4 = (bf16[208,1920]{1,0:T(8,128)(2,1)}, bf16[208,1920]{1,0:T(8,128)(2,1)}, u32[]{:S(2)}, u32[]{:S(2)}) collective-permute-start(bf16[208,1920]{1,0:T(8,128)(2,1)} %collective-permute-done.refs_1_), channel_id=1, source_target_pairs={{0,4},{4,0},{1,5},{5,1},{2,6},{6,2},{3,7},{7,3},{8,12},{12,8},{9,1... | collective-permute-start | bytes 2396168 | tf_op jit(solution)/shard_map/ppermute | solution.py:868
  96.3 56.5 %collective-permute-start.21 = (bf16[384,1536]{1,0:T(8,128)(2,1)S(1)}, bf16[384,1536]{1,0:T(8,128)(2,1)}, u32[]{:S(2)}, u32[]{:S(2)}) collective-permute-start(bf16[384,1536]{1,0:T(8,128)(2,1)S(1)} %copy-done.25), channel_id=1, source_target_pairs={{0,4},{4,0},{1,5},{5,1},{2,6},{6,2},{3,7},{7,3},{8,12},{12,8},{9,1... | collective-permute-start | bytes 3538952 | tf_op jit(solution)/shard_map/ppermute | solution.py:868
  121.5 28.7 %collective-permute-start.16 = (bf16[2,128,1536]{2,1,0:T(8,128)(2,1)S(1)}, bf16[2,128,1536]{2,1,0:T(8,128)(2,1)}, u32[]{:S(2)}, u32[]{:S(2)}) collective-permute-start(bf16[2,128,1536]{2,1,0:T(8,128)(2,1)S(1)} %pad_maximum_fusion.7.refs_4_), channel_id=1, source_target_pairs={{0,8},{8,0},{16,24},{24,16},{1,9},{9,1},{17,25},{25,17},{2,10},{10... | collective-permute-start | bytes 2359304 | tf_op jit(solution)/shard_map/ppermute | solution.py:864
  195.6 29.7 %collective-permute-start.29 = (bf16[1,128,1536]{2,1,0:T(8,128)(2,1)}, bf16[1,128,1536]{2,1,0:T(8,128)(2,1)}, u32[]{:S(2)}, u32[]{:S(2)}) collective-permute-start(bf16[1,128,1536]{2,1,0:T(8,128)(2,1)} %slice.363), channel_id=1, source_target_pairs={{0,8},{8,0},{16,24},{24,16},{1,9},{9,1},{17,25},{25,17},{2,10},{10... | collective-permute-start | bytes 1179656 | tf_op jit(solution)/shard_map/ppermute | solution.py:864
  237.9 79.6 %collective-permute-start.26 = (bf16[2,128,1536]{2,1,0:T(8,128)(2,1)}, bf16[2,128,1536]{2,1,0:T(8,128)(2,1)}, u32[]{:S(2)}, u32[]{:S(2)}) collective-permute-start(bf16[2,128,1536]{2,1,0:T(8,128)(2,1)} %bitcast.14), channel_id=1, source_target_pairs={{0,16},{8,24},{16,0},{24,8},{1,17},{9,25},{17,1},{25,9},{2,18},{10... | collective-permute-start | bytes 2359304 | tf_op jit(solution)/shard_map/ppermute | solution.py:864
  239.2 78.3 %collective-permute-start.27 = (bf16[2,128,1536]{2,1,0:T(8,128)(2,1)}, bf16[2,128,1536]{2,1,0:T(8,128)(2,1)}, u32[]{:S(2)}, u32[]{:S(2)}) collective-permute-start(bf16[2,128,1536]{2,1,0:T(8,128)(2,1)} %bitcast.15), channel_id=1, source_target_pairs={{0,8},{8,0},{16,24},{24,16},{1,9},{9,1},{17,25},{25,17},{2,10},{10... | collective-permute-start | bytes 2359304 | tf_op jit(solution)/shard_map/ppermute | solution.py:864
  277.7 42.6 %collective-permute-start.34 = (bf16[2,128,1536]{2,1,0:T(8,128)(2,1)}, bf16[2,128,1536]{2,1,0:T(8,128)(2,1)}, u32[]{:S(2)}, u32[]{:S(2)}) collective-permute-start(bf16[2,128,1536]{2,1,0:T(8,128)(2,1)} %bitcast.24), channel_id=1, source_target_pairs={{0,16},{8,24},{16,0},{24,8},{1,17},{9,25},{17,1},{25,9},{2,18},{10... | collective-permute-start | bytes 2359304 | tf_op jit(solution)/shard_map/ppermute | solution.py:864
  283.5 36.9 %collective-permute-start.35 = (bf16[2,128,1536]{2,1,0:T(8,128)(2,1)S(1)}, bf16[2,128,1536]{2,1,0:T(8,128)(2,1)}, u32[]{:S(2)}, u32[]{:S(2)}) collective-permute-start(bf16[2,128,1536]{2,1,0:T(8,128)(2,1)S(1)} %bitcast.122), channel_id=1, source_target_pairs={{0,8},{8,0},{16,24},{24,16},{1,9},{9,1},{17,25},{25,17},{2,10},{10... | collective-permute-start | bytes 2359304 | tf_op jit(solution)/shard_map/ppermute | solution.py:864
  288.8 115.2 %all-gather.3.cloned.1.call-start = ((), (), s32[]{:S(2)}) async-start(), calls=%async_computation.3 | async-start | bytes 2949120 | tf_op jit(solution)/shard_map/all_gather | solution.py:965
  319.6 44.2 %collective-permute-start.37 = (bf16[1,128,1536]{2,1,0:T(8,128)(2,1)}, bf16[1,128,1536]{2,1,0:T(8,128)(2,1)}, u32[]{:S(2)}, u32[]{:S(2)}) collective-permute-start(bf16[1,128,1536]{2,1,0:T(8,128)(2,1)} %slice.486), channel_id=1, source_target_pairs={{0,16},{8,24},{16,0},{24,8},{1,17},{9,25},{17,1},{25,9},{2,18},{10... | collective-permute-start | bytes 1179656 | tf_op jit(solution)/shard_map/ppermute | solution.py:864
  323.4 41.6 %collective-permute-start.38 = (bf16[1,128,1536]{2,1,0:T(8,128)(2,1)}, bf16[1,128,1536]{2,1,0:T(8,128)(2,1)}, u32[]{:S(2)}, u32[]{:S(2)}) collective-permute-start(bf16[1,128,1536]{2,1,0:T(8,128)(2,1)} %slice.485), channel_id=1, source_target_pairs={{0,16},{8,24},{16,0},{24,8},{1,17},{9,25},{17,1},{25,9},{2,18},{10... | collective-permute-start | bytes 1179656 | tf_op jit(solution)/shard_map/ppermute | solution.py:864
  353.3 125.6 %reduce-scatter.5.cloned.1.call-start = ((), (), s32[]{:S(2)}) async-start(), calls=%async_computation.4 | async-start | bytes 2211840 | tf_op jit(solution)/shard_map/reduce_scatter | solution.py:961
  374.9 37.4 %collective-permute-start.41 = (bf16[2,128,1536]{2,1,0:T(8,128)(2,1)}, bf16[2,128,1536]{2,1,0:T(8,128)(2,1)}, u32[]{:S(2)}, u32[]{:S(2)}) collective-permute-start(bf16[2,128,1536]{2,1,0:T(8,128)(2,1)} %bitcast.30), channel_id=1, source_target_pairs={{0,16},{8,24},{16,0},{24,8},{1,17},{9,25},{17,1},{25,9},{2,18},{10... | collective-permute-start | bytes 2359304 | tf_op jit(solution)/shard_map/ppermute | solution.py:864
  375.9 36.4 %collective-permute-start.42 = (bf16[2,128,1536]{2,1,0:T(8,128)(2,1)}, bf16[2,128,1536]{2,1,0:T(8,128)(2,1)}, u32[]{:S(2)}, u32[]{:S(2)}) collective-permute-start(bf16[2,128,1536]{2,1,0:T(8,128)(2,1)} %bitcast.31), channel_id=1, source_target_pairs={{0,8},{8,0},{16,24},{24,16},{1,9},{9,1},{17,25},{25,17},{2,10},{10... | collective-permute-start | bytes 2359304 | tf_op jit(solution)/shard_map/ppermute | solution.py:864
  414.5 49.5 %collective-permute-start.47 = (bf16[1,128,1536]{2,1,0:T(8,128)(2,1)}, bf16[1,128,1536]{2,1,0:T(8,128)(2,1)}, u32[]{:S(2)}, u32[]{:S(2)}) collective-permute-start(bf16[1,128,1536]{2,1,0:T(8,128)(2,1)} %slice.483), channel_id=1, source_target_pairs={{0,16},{8,24},{16,0},{24,8},{1,17},{9,25},{17,1},{25,9},{2,18},{10... | collective-permute-start | bytes 1179656 | tf_op jit(solution)/shard_map/ppermute | solution.py:864
  418.8 45.3 %collective-permute-start.46 = (bf16[1,128,1536]{2,1,0:T(8,128)(2,1)S(1)}, bf16[1,128,1536]{2,1,0:T(8,128)(2,1)}, u32[]{:S(2)}, u32[]{:S(2)}) collective-permute-start(bf16[1,128,1536]{2,1,0:T(8,128)(2,1)S(1)} %slice.484), channel_id=1, source_target_pairs={{0,8},{8,0},{16,24},{24,16},{1,9},{9,1},{17,25},{25,17},{2,10},{10... | collective-permute-start | bytes 1179656 | tf_op jit(solution)/shard_map/ppermute | solution.py:864
  430.7 92.1 %all-gather.5.cloned.1.call-start = ((), (), s32[]{:S(2)}) async-start(), calls=%async_computation.5 | async-start | bytes 1658880 | tf_op jit(solution)/shard_map/all_gather | solution.py:965
  (120 other events, 1203.6 us)
Sparse Core Ops, SparseCore 0:
  288.9 47.8 reduce-scatter.2
  353.4 50.5 all-gather.2
  430.9 38.3 reduce-scatter.4
  491.4 31.4 all-gather.4
